TPU v7x, 256 devices: a whole 4x4x8 slice. The times are simulated.
256 devices in a mesh: layer: 4 (over y), tile: 64 (over z, x, core).
Axes of the slice: x: 4, y: 4, z: 8, core: 2. Of those that a mesh axis runs over, the one named last changes fastest.
Arguments:
- source_field: float32 [16, 2, 16, 64, 512], P('layer', None, None, 'tile'), may hold values from -4 to 4
- wave_shift: float32 [16, 2, 64, 512], P('layer', None, 'tile'), may hold values from 0.2 to 2
- frontal_blocks: bfloat16 [4, 256, 8, 2, 128, 128], P('layer', 'tile'), may hold values from -0.125 to 0.125
- block_columns: int32 [4, 256, 8], P('layer', 'tile'), may hold values from 0 to 8
Outputs:
- solution_field: float32 [16, 2, 16, 64, 512], P('layer', None, None, 'tile')
- residual_field: float32 [16, 2, 16, 64, 512], P('layer', None, None, 'tile')
Inputs may be any that keep to these rules, and one draw needn't show every extreme that they name: `block_columns`: a value c in block row b refers to block b + c - 4; where that lies outside the plane the block adds nothing.
All inputs are finite; a program needn't handle non-finite values.
Results may differ from a plain program's by a relative error of at most 0.022.
Values may be sent and summed in bfloat16 or wider, within the bound.
A program may use at most 64 MiB of HBM per device.

v0:
```python
import jax
import jax.numpy as jnp
from jax import lax
from jax.sharding import PartitionSpec as P

REACH = 4


def with_halo(block, sides, width):
    for axis, dim in sides:
        count = lax.axis_size(axis)
        forward = [(i, i + 1) for i in range(count - 1)]
        backward = [(target, source) for source, target in forward]
        low = lax.ppermute(
            lax.slice_in_dim(block, block.shape[dim] - width, None, axis=dim), axis, forward
        )
        high = lax.ppermute(lax.slice_in_dim(block, 0, width, axis=dim), axis, backward)
        block = jnp.concatenate([low, block, high], axis=dim)
    return block


def from_behind(block, axis, distance):
    devices = range(lax.axis_size(axis))
    route = [(i - distance, i) for i in devices if i - distance in devices]
    return lax.ppermute(block, axis, route)


def apply_front(vector, frontal, columns):
    count = frontal.shape[0]
    block_size = frontal.shape[-1]
    width_cols = vector.shape[1]
    blocks = vector.astype(jnp.bfloat16).reshape(2, width_cols, count, block_size)
    extended = with_halo(blocks, (("tile", 2),), REACH)
    where_from = jnp.arange(count, dtype=jnp.int32)[:, None] + columns
    picked = extended[:, :, where_from]
    pattern = "rbkj,bkji->rbi"

    def product_of(operand, matrix):
        return jnp.einsum(pattern, operand, matrix, preferred_element_type=jnp.float32)

    real_part = product_of(picked[0], frontal[:, :, 0]) - product_of(picked[1], frontal[:, :, 1])
    imag_part = product_of(picked[0], frontal[:, :, 1]) + product_of(picked[1], frontal[:, :, 0])
    return jnp.stack([real_part, imag_part]).reshape(vector.shape)


def sweep_layer(source_part, incoming, frontal, columns):
    previous = incoming
    results = []
    for plane_index in range(source_part.shape[0]):
        previous = apply_front(source_part[plane_index] + previous, frontal, columns)
        results.append(previous)
    return (jnp.stack(results), previous)


def residual_of(solution, source_field, wave_shift):
    padded = with_halo(solution, (("layer", 0), ("tile", 3)), 1)
    center = padded[1:-1, :, :, 1:-1]
    beside = padded[2:, :, :, 1:-1] + padded[:-2, :, :, 1:-1]
    beside = beside + padded[1:-1, :, :, 2:] + padded[1:-1, :, :, :-2]
    widened = jnp.pad(center, ((0, 0), (0, 0), (0, 0), (0, 0), (1, 1)))
    beside = beside + widened[..., 2:] + widened[..., :-2]
    shift_re = wave_shift[:, 0][:, None]
    shift_im = wave_shift[:, 1][:, None]
    value_re = (6.0 - shift_re) * center[:, 0] + shift_im * center[:, 1] - beside[:, 0]
    value_im = (6.0 - shift_re) * center[:, 1] - shift_im * center[:, 0] - beside[:, 1]
    return source_field - jnp.stack([value_re, value_im], axis=1)


def per_device(source_field, wave_shift, frontal_blocks, block_columns):
    frontal = frontal_blocks[0]
    pattern_cols = block_columns[0]
    layer_index = lax.axis_index("layer")
    layer_count = lax.axis_size("layer")
    total_cols = source_field.shape[2]
    groups_used = 1
    group_cols = total_cols // groups_used
    solution = jnp.zeros_like(source_field)
    plane_shape = source_field.shape[3:]
    outgoing = jnp.zeros((2, group_cols) + plane_shape, jnp.float32)
    for section_index in range(layer_count + groups_used - 1):
        incoming = from_behind(outgoing, "layer", 1)
        offset = section_index - layer_index
        active = (offset >= 0) & (offset < groups_used)
        planes, outgoing = sweep_layer(source_field, incoming, frontal, pattern_cols)
        current = solution
        solution = jnp.where(active, planes, current)
    residual = residual_of(solution, source_field, wave_shift)
    return (solution, residual)


def solution(mesh):
    placed = (
        P("layer", None, None, "tile", None),
        P("layer", None, "tile", None),
        P("layer", "tile", None, None, None, None),
        P("layer", "tile", None),
    )
    return jax.shard_map(
        per_device,
        mesh=mesh,
        in_specs=placed,
        out_specs=(P("layer", None, None, "tile", None), P("layer", None, None, "tile", None)),
        check_vma=False,
    )
```

profile of v0, /device:TPU:127, one launch (start us, length us, event | category | flops | bytes accessed | tf_op | source)
XLA Modules:
  0.0 248.3 jit_solution(5888902718667125120)
XLA Ops:
  3.7 2.0 collective-permute-done
  5.7 6.4 %collective-permute-start.1 = (bf16[2,16,4,128]{3,1,2,0:T(8,128)(2,1)S(1)}, bf16[2,16,4,128]{3,1,2,0:T(8,128)(2,1)S(1)}, u32[]{:S(2)}, u32[]{:S(2)}) collective-permute-start(bf16[2,16,4,128]{3,1,2,0:T(8,128)(2,1)S(1)} %copy.91), channel_id=1, source_target_pairs={{0,1},{1,2},{2,3},{3,4},{4,5},{5,6},{6,7},{7,8},{8,9},{9,10},{10,1... | collective-permute-start | bytes 98312 | tf_op jit(solution)/shard_map/ppermute | solution.py:14
  12.1 1.9 collective-permute-start.2
  15.8 4.9 %collective-permute-done.2 = bf16[2,16,4,128]{3,1,2,0:T(8,128)(2,1)S(1)} collective-permute-done((bf16[2,16,4,128]{3,1,2,0:T(8,128)(2,1)S(1)}, bf16[2,16,4,128]{3,1,2,0:T(8,128)(2,1)S(1)}, u32[]{:S(2)}, u32[]{:S(2)}) %collective-permute-start.2) | collective-permute-done | bytes 32800 | tf_op jit(solution)/shard_map/ppermute | solution.py:17
  22.4 2.1 collective-permute-start.3
  24.5 2.2 collective-permute-start.4
  26.7 6.3 %collective-permute-done.4 = bf16[2,16,4,128]{3,1,2,0:T(8,128)(2,1)S(1)} collective-permute-done((bf16[2,16,4,128]{3,1,2,0:T(8,128)(2,1)S(1)}, bf16[2,16,4,128]{3,1,2,0:T(8,128)(2,1)S(1)}, u32[]{:S(2)}, u32[]{:S(2)}) %collective-permute-start.4) | collective-permute-done | bytes 32800 | tf_op jit(solution)/shard_map/ppermute | solution.py:17
  34.8 1.9 collective-permute-start.5
  36.7 2.4 collective-permute-start.6
  39.1 6.1 %collective-permute-done.6 = bf16[2,16,4,128]{3,1,2,0:T(8,128)(2,1)S(1)} collective-permute-done((bf16[2,16,4,128]{3,1,2,0:T(8,128)(2,1)S(1)}, bf16[2,16,4,128]{3,1,2,0:T(8,128)(2,1)S(1)}, u32[]{:S(2)}, u32[]{:S(2)}) %collective-permute-start.6) | collective-permute-done | bytes 32800 | tf_op jit(solution)/shard_map/ppermute | solution.py:17
  47.0 1.9 collective-permute-start.7
  48.9 2.4 collective-permute-start.8
  51.3 6.1 %collective-permute-done.8 = bf16[2,16,4,128]{3,1,2,0:T(8,128)(2,1)S(1)} collective-permute-done((bf16[2,16,4,128]{3,1,2,0:T(8,128)(2,1)S(1)}, bf16[2,16,4,128]{3,1,2,0:T(8,128)(2,1)S(1)}, u32[]{:S(2)}, u32[]{:S(2)}) %collective-permute-start.8) | collective-permute-done | bytes 32800 | tf_op jit(solution)/shard_map/ppermute | solution.py:17
  60.6 3.7 %collective-permute-done.9 = f32[2,16,1,512]{3,1,2,0:T(8,128)S(1)} collective-permute-done((f32[2,16,1,512]{3,1,2,0:T(8,128)S(1)}, f32[2,16,1,512]{3,1,2,0:T(8,128)S(1)}, u32[]{:S(2)}, u32[]{:S(2)}) %collective-permute-start.9) | collective-permute-done | bytes 65568 | tf_op jit(solution)/shard_map/ppermute | solution.py:25
  64.3 3.1 %collective-permute-start.10 = (bf16[2,16,4,128]{3,1,2,0:T(8,128)(2,1)S(1)}, bf16[2,16,4,128]{3,1,2,0:T(8,128)(2,1)S(1)}, u32[]{:S(2)}, u32[]{:S(2)}) collective-permute-start(bf16[2,16,4,128]{3,1,2,0:T(8,128)(2,1)S(1)} %copy.104), channel_id=1, source_target_pairs={{0,1},{1,2},{2,3},{3,4},{4,5},{5,6},{6,7},{7,8},{8,9},{9,10},{10,1... | collective-permute-start | bytes 98312 | tf_op jit(solution)/shard_map/ppermute | solution.py:14
  67.4 1.9 collective-permute-start.11
  69.3 6.6 %collective-permute-done.11 = bf16[2,16,4,128]{3,1,2,0:T(8,128)(2,1)S(1)} collective-permute-done((bf16[2,16,4,128]{3,1,2,0:T(8,128)(2,1)S(1)}, bf16[2,16,4,128]{3,1,2,0:T(8,128)(2,1)S(1)}, u32[]{:S(2)}, u32[]{:S(2)}) %collective-permute-start.11) | collective-permute-done | bytes 32800 | tf_op jit(solution)/shard_map/ppermute | solution.py:17
  77.7 1.9 collective-permute-start.12
  79.6 2.4 collective-permute-start.13
  82.0 6.1 %collective-permute-done.13 = bf16[2,16,4,128]{3,1,2,0:T(8,128)(2,1)S(1)} collective-permute-done((bf16[2,16,4,128]{3,1,2,0:T(8,128)(2,1)S(1)}, bf16[2,16,4,128]{3,1,2,0:T(8,128)(2,1)S(1)}, u32[]{:S(2)}, u32[]{:S(2)}) %collective-permute-start.13) | collective-permute-done | bytes 32800 | tf_op jit(solution)/shard_map/ppermute | solution.py:17
  91.8 2.4 collective-permute-start.15
  94.2 6.1 %collective-permute-done.15 = bf16[2,16,4,128]{3,1,2,0:T(8,128)(2,1)S(1)} collective-permute-done((bf16[2,16,4,128]{3,1,2,0:T(8,128)(2,1)S(1)}, bf16[2,16,4,128]{3,1,2,0:T(8,128)(2,1)S(1)}, u32[]{:S(2)}, u32[]{:S(2)}) %collective-permute-start.15) | collective-permute-done | bytes 32800 | tf_op jit(solution)/shard_map/ppermute | solution.py:17
  104.0 2.4 collective-permute-start.17
  106.4 6.1 %collective-permute-done.17 = bf16[2,16,4,128]{3,1,2,0:T(8,128)(2,1)S(1)} collective-permute-done((bf16[2,16,4,128]{3,1,2,0:T(8,128)(2,1)S(1)}, bf16[2,16,4,128]{3,1,2,0:T(8,128)(2,1)S(1)}, u32[]{:S(2)}, u32[]{:S(2)}) %collective-permute-start.17) | collective-permute-done | bytes 32800 | tf_op jit(solution)/shard_map/ppermute | solution.py:17
  115.7 3.7 %collective-permute-done.18 = f32[2,16,1,512]{3,1,2,0:T(8,128)S(1)} collective-permute-done((f32[2,16,1,512]{3,1,2,0:T(8,128)S(1)}, f32[2,16,1,512]{3,1,2,0:T(8,128)S(1)}, u32[]{:S(2)}, u32[]{:S(2)}) %collective-permute-start.18) | collective-permute-done | bytes 65568 | tf_op jit(solution)/shard_map/ppermute | solution.py:25
  119.4 3.1 %collective-permute-start.19 = (bf16[2,16,4,128]{3,1,2,0:T(8,128)(2,1)S(1)}, bf16[2,16,4,128]{3,1,2,0:T(8,128)(2,1)S(1)}, u32[]{:S(2)}, u32[]{:S(2)}) collective-permute-start(bf16[2,16,4,128]{3,1,2,0:T(8,128)(2,1)S(1)} %copy.116), channel_id=1, source_target_pairs={{0,1},{1,2},{2,3},{3,4},{4,5},{5,6},{6,7},{7,8},{8,9},{9,10},{10,1... | collective-permute-start | bytes 98312 | tf_op jit(solution)/shard_map/ppermute | solution.py:14
  124.4 6.6 %collective-permute-done.20 = bf16[2,16,4,128]{3,1,2,0:T(8,128)(2,1)S(1)} collective-permute-done((bf16[2,16,4,128]{3,1,2,0:T(8,128)(2,1)S(1)}, bf16[2,16,4,128]{3,1,2,0:T(8,128)(2,1)S(1)}, u32[]{:S(2)}, u32[]{:S(2)}) %collective-permute-start.20) | collective-permute-done | bytes 32800 | tf_op jit(solution)/shard_map/ppermute | solution.py:17
  134.7 2.4 collective-permute-start.22
  137.1 6.1 %collective-permute-done.22 = bf16[2,16,4,128]{3,1,2,0:T(8,128)(2,1)S(1)} collective-permute-done((bf16[2,16,4,128]{3,1,2,0:T(8,128)(2,1)S(1)}, bf16[2,16,4,128]{3,1,2,0:T(8,128)(2,1)S(1)}, u32[]{:S(2)}, u32[]{:S(2)}) %collective-permute-start.22) | collective-permute-done | bytes 32800 | tf_op jit(solution)/shard_map/ppermute | solution.py:17
  146.9 2.4 collective-permute-start.24
  149.4 6.1 %collective-permute-done.24 = bf16[2,16,4,128]{3,1,2,0:T(8,128)(2,1)S(1)} collective-permute-done((bf16[2,16,4,128]{3,1,2,0:T(8,128)(2,1)S(1)}, bf16[2,16,4,128]{3,1,2,0:T(8,128)(2,1)S(1)}, u32[]{:S(2)}, u32[]{:S(2)}) %collective-permute-start.24) | collective-permute-done | bytes 32800 | tf_op jit(solution)/shard_map/ppermute | solution.py:17
  157.2 1.9 collective-permute-start.25
  159.1 2.6 %collective-permute-start.26 = (bf16[2,16,4,128]{3,1,2,0:T(8,128)(2,1)S(1)}, bf16[2,16,4,128]{3,1,2,0:T(8,128)(2,1)S(1)}, u32[]{:S(2)}, u32[]{:S(2)}) collective-permute-start(bf16[2,16,4,128]{3,1,2,0:T(8,128)(2,1)S(1)} %fusion.51), channel_id=1, source_target_pairs={{1,0},{2,1},{3,2},{4,3},{5,4},{6,5},{7,6},{8,7},{9,8},{10,9},{11,1... | collective-permute-start | bytes 98312 | tf_op jit(solution)/shard_map/ppermute | solution.py:17
  161.7 5.9 %collective-permute-done.26 = bf16[2,16,4,128]{3,1,2,0:T(8,128)(2,1)S(1)} collective-permute-done((bf16[2,16,4,128]{3,1,2,0:T(8,128)(2,1)S(1)}, bf16[2,16,4,128]{3,1,2,0:T(8,128)(2,1)S(1)}, u32[]{:S(2)}, u32[]{:S(2)}) %collective-permute-start.26) | collective-permute-done | bytes 32800 | tf_op jit(solution)/shard_map/ppermute | solution.py:17
  170.8 3.7 %collective-permute-done.27 = f32[2,16,1,512]{3,1,2,0:T(8,128)S(1)} collective-permute-done((f32[2,16,1,512]{3,1,2,0:T(8,128)S(1)}, f32[2,16,1,512]{3,1,2,0:T(8,128)S(1)}, u32[]{:S(2)}, u32[]{:S(2)}) %collective-permute-start.27) | collective-permute-done | bytes 65568 | tf_op jit(solution)/shard_map/ppermute | solution.py:25
  174.6 3.1 %collective-permute-start.28 = (bf16[2,16,4,128]{3,1,2,0:T(8,128)(2,1)S(1)}, bf16[2,16,4,128]{3,1,2,0:T(8,128)(2,1)S(1)}, u32[]{:S(2)}, u32[]{:S(2)}) collective-permute-start(bf16[2,16,4,128]{3,1,2,0:T(8,128)(2,1)S(1)} %copy.128), channel_id=1, source_target_pairs={{0,1},{1,2},{2,3},{3,4},{4,5},{5,6},{6,7},{7,8},{8,9},{9,10},{10,1... | collective-permute-start | bytes 98312 | tf_op jit(solution)/shard_map/ppermute | solution.py:14
  177.7 1.9 collective-permute-start.29
  179.6 6.6 %collective-permute-done.29 = bf16[2,16,4,128]{3,1,2,0:T(8,128)(2,1)S(1)} collective-permute-done((bf16[2,16,4,128]{3,1,2,0:T(8,128)(2,1)S(1)}, bf16[2,16,4,128]{3,1,2,0:T(8,128)(2,1)S(1)}, u32[]{:S(2)}, u32[]{:S(2)}) %collective-permute-start.29) | collective-permute-done | bytes 32800 | tf_op jit(solution)/shard_map/ppermute | solution.py:17
  189.9 2.4 collective-permute-start.31
  192.3 6.1 %collective-permute-done.31 = bf16[2,16,4,128]{3,1,2,0:T(8,128)(2,1)S(1)} collective-permute-done((bf16[2,16,4,128]{3,1,2,0:T(8,128)(2,1)S(1)}, bf16[2,16,4,128]{3,1,2,0:T(8,128)(2,1)S(1)}, u32[]{:S(2)}, u32[]{:S(2)}) %collective-permute-start.31) | collective-permute-done | bytes 32800 | tf_op jit(solution)/shard_map/ppermute | solution.py:17
  202.1 2.4 collective-permute-start.33
  204.5 6.1 %collective-permute-done.33 = bf16[2,16,4,128]{3,1,2,0:T(8,128)(2,1)S(1)} collective-permute-done((bf16[2,16,4,128]{3,1,2,0:T(8,128)(2,1)S(1)}, bf16[2,16,4,128]{3,1,2,0:T(8,128)(2,1)S(1)}, u32[]{:S(2)}, u32[]{:S(2)}) %collective-permute-start.33) | collective-permute-done | bytes 32800 | tf_op jit(solution)/shard_map/ppermute | solution.py:17
  214.3 2.4 collective-permute-start.35
  224.9 2.5 %collective-permute-start.36 = (f32[1,2,16,1,512]{4,2,3,1,0:T(8,128)S(1)}, f32[1,2,16,1,512]{4,2,3,1,0:T(8,128)S(1)}, u32[]{:S(2)}, u32[]{:S(2)}) collective-permute-start(f32[1,2,16,1,512]{4,2,3,1,0:T(8,128)S(1)} %get-tuple-element.9), channel_id=1, source_target_pairs={{64,0},{128,64},{192,128},{65,1},{129,65},{193,129},{66,2},{130,66... | collective-permute-start | bytes 196616 | tf_op jit(solution)/shard_map/ppermute | solution.py:17
  229.1 4.2 %collective-permute-done.37 = f32[1,2,16,1,512]{4,2,3,1,0:T(8,128)S(1)} collective-permute-done((f32[1,2,16,1,512]{4,2,3,1,0:T(8,128)S(1)}, f32[1,2,16,1,512]{4,2,3,1,0:T(8,128)S(1)}, u32[]{:S(2)}, u32[]{:S(2)}) %collective-permute-start.37) | collective-permute-done | bytes 65568 | tf_op jit(solution)/shard_map/ppermute | solution.py:14
  233.4 2.4 collective-permute-start.38
  235.8 6.5 %collective-permute-start.39 = (f32[6,2,16,1,512]{4,2,3,1,0:T(8,128)S(1)}, f32[6,2,16,1,512]{4,2,3,1,0:T(8,128)S(1)}, u32[]{:S(2)}, u32[]{:S(2)}) collective-permute-start(f32[6,2,16,1,512]{4,2,3,1,0:T(8,128)S(1)} %pad_maximum_fusion), channel_id=1, source_target_pairs={{0,1},{1,2},{2,3},{3,4},{4,5},{5,6},{6,7},{7,8},{8,9},{9,10},{10,1... | collective-permute-start | bytes 1179656 | tf_op jit(solution)/shard_map/ppermute | solution.py:14
  243.3 2.5 %collective-permute-done.38 = f32[6,2,16,1,512]{4,2,3,1,0:T(8,128)S(1)} collective-permute-done((f32[6,2,16,1,512]{4,2,3,1,0:T(8,128)S(1)}, f32[6,2,16,1,512]{4,2,3,1,0:T(8,128)S(1)}, u32[]{:S(2)}, u32[]{:S(2)}) %collective-permute-start.38) | collective-permute-done | bytes 393248 | tf_op jit(solution)/shard_map/ppermute | solution.py:17
  (295 shorter events, 62.6 us)
Async XLA Ops:
  0.6 5.0 %collective-permute-start = (f32[2,16,1,512]{3,1,2,0:T(8,128)S(1)}, f32[2,16,1,512]{3,1,2,0:T(8,128)S(1)}, u32[]{:S(2)}, u32[]{:S(2)}) collective-permute-start(f32[2,16,1,512]{3,1,2,0:T(8,128)S(1)} %broadcast_in_dim.4), channel_id=1, source_target_pairs={{0,64},{64,128},{128,192},{1,65},{65,129},{129,193},{2,66},{66,130... | collective-permute-start | bytes 196616 | tf_op jit(solution)/shard_map/ppermute | solution.py:25
  5.7 10.1 %collective-permute-start.1 = (bf16[2,16,4,128]{3,1,2,0:T(8,128)(2,1)S(1)}, bf16[2,16,4,128]{3,1,2,0:T(8,128)(2,1)S(1)}, u32[]{:S(2)}, u32[]{:S(2)}) collective-permute-start(bf16[2,16,4,128]{3,1,2,0:T(8,128)(2,1)S(1)} %copy.91), channel_id=1, source_target_pairs={{0,1},{1,2},{2,3},{3,4},{4,5},{5,6},{6,7},{7,8},{8,9},{9,10},{10,1... | collective-permute-start | bytes 98312 | tf_op jit(solution)/shard_map/ppermute | solution.py:14
  12.1 8.6 %collective-permute-start.2 = (bf16[2,16,4,128]{3,1,2,0:T(8,128)(2,1)S(1)}, bf16[2,16,4,128]{3,1,2,0:T(8,128)(2,1)S(1)}, u32[]{:S(2)}, u32[]{:S(2)}) collective-permute-start(bf16[2,16,4,128]{3,1,2,0:T(8,128)(2,1)S(1)} %copy.91), channel_id=1, source_target_pairs={{1,0},{2,1},{3,2},{4,3},{5,4},{6,5},{7,6},{8,7},{9,8},{10,9},{11,1... | collective-permute-start | bytes 98312 | tf_op jit(solution)/shard_map/ppermute | solution.py:17
  22.4 4.3 %collective-permute-start.3 = (bf16[2,16,4,128]{3,1,2,0:T(8,128)(2,1)S(1)}, bf16[2,16,4,128]{3,1,2,0:T(8,128)(2,1)S(1)}, u32[]{:S(2)}, u32[]{:S(2)}) collective-permute-start(bf16[2,16,4,128]{3,1,2,0:T(8,128)(2,1)S(1)} %fusion.43), channel_id=1, source_target_pairs={{0,1},{1,2},{2,3},{3,4},{4,5},{5,6},{6,7},{7,8},{8,9},{9,10},{10,1... | collective-permute-start | bytes 98312 | tf_op jit(solution)/shard_map/ppermute | solution.py:14
  24.5 8.6 %collective-permute-start.4 = (bf16[2,16,4,128]{3,1,2,0:T(8,128)(2,1)S(1)}, bf16[2,16,4,128]{3,1,2,0:T(8,128)(2,1)S(1)}, u32[]{:S(2)}, u32[]{:S(2)}) collective-permute-start(bf16[2,16,4,128]{3,1,2,0:T(8,128)(2,1)S(1)} %fusion.43), channel_id=1, source_target_pairs={{1,0},{2,1},{3,2},{4,3},{5,4},{6,5},{7,6},{8,7},{9,8},{10,9},{11,1... | collective-permute-start | bytes 98312 | tf_op jit(solution)/shard_map/ppermute | solution.py:17
  34.8 4.3 %collective-permute-start.5 = (bf16[2,16,4,128]{3,1,2,0:T(8,128)(2,1)S(1)}, bf16[2,16,4,128]{3,1,2,0:T(8,128)(2,1)S(1)}, u32[]{:S(2)}, u32[]{:S(2)}) collective-permute-start(bf16[2,16,4,128]{3,1,2,0:T(8,128)(2,1)S(1)} %fusion.44), channel_id=1, source_target_pairs={{0,1},{1,2},{2,3},{3,4},{4,5},{5,6},{6,7},{7,8},{8,9},{9,10},{10,1... | collective-permute-start | bytes 98312 | tf_op jit(solution)/shard_map/ppermute | solution.py:14
  36.7 8.6 %collective-permute-start.6 = (bf16[2,16,4,128]{3,1,2,0:T(8,128)(2,1)S(1)}, bf16[2,16,4,128]{3,1,2,0:T(8,128)(2,1)S(1)}, u32[]{:S(2)}, u32[]{:S(2)}) collective-permute-start(bf16[2,16,4,128]{3,1,2,0:T(8,128)(2,1)S(1)} %fusion.44), channel_id=1, source_target_pairs={{1,0},{2,1},{3,2},{4,3},{5,4},{6,5},{7,6},{8,7},{9,8},{10,9},{11,1... | collective-permute-start | bytes 98312 | tf_op jit(solution)/shard_map/ppermute | solution.py:17
  47.0 4.3 %collective-permute-start.7 = (bf16[2,16,4,128]{3,1,2,0:T(8,128)(2,1)S(1)}, bf16[2,16,4,128]{3,1,2,0:T(8,128)(2,1)S(1)}, u32[]{:S(2)}, u32[]{:S(2)}) collective-permute-start(bf16[2,16,4,128]{3,1,2,0:T(8,128)(2,1)S(1)} %fusion.45), channel_id=1, source_target_pairs={{0,1},{1,2},{2,3},{3,4},{4,5},{5,6},{6,7},{7,8},{8,9},{9,10},{10,1... | collective-permute-start | bytes 98312 | tf_op jit(solution)/shard_map/ppermute | solution.py:14
  48.9 8.6 %collective-permute-start.8 = (bf16[2,16,4,128]{3,1,2,0:T(8,128)(2,1)S(1)}, bf16[2,16,4,128]{3,1,2,0:T(8,128)(2,1)S(1)}, u32[]{:S(2)}, u32[]{:S(2)}) collective-permute-start(bf16[2,16,4,128]{3,1,2,0:T(8,128)(2,1)S(1)} %fusion.45), channel_id=1, source_target_pairs={{1,0},{2,1},{3,2},{4,3},{5,4},{6,5},{7,6},{8,7},{9,8},{10,9},{11,1... | collective-permute-start | bytes 98312 | tf_op jit(solution)/shard_map/ppermute | solution.py:17
  59.3 5.0 %collective-permute-start.9 = (f32[2,16,1,512]{3,1,2,0:T(8,128)S(1)}, f32[2,16,1,512]{3,1,2,0:T(8,128)S(1)}, u32[]{:S(2)}, u32[]{:S(2)}) collective-permute-start(f32[2,16,1,512]{3,1,2,0:T(8,128)S(1)} %pad_maximum_fusion.19), channel_id=1, source_target_pairs={{0,64},{64,128},{128,192},{1,65},{65,129},{129,193},{2,66},{66,130... | collective-permute-start | bytes 196616 | tf_op jit(solution)/shard_map/ppermute | solution.py:25
  64.3 5.0 %collective-permute-start.10 = (bf16[2,16,4,128]{3,1,2,0:T(8,128)(2,1)S(1)}, bf16[2,16,4,128]{3,1,2,0:T(8,128)(2,1)S(1)}, u32[]{:S(2)}, u32[]{:S(2)}) collective-permute-start(bf16[2,16,4,128]{3,1,2,0:T(8,128)(2,1)S(1)} %copy.104), channel_id=1, source_target_pairs={{0,1},{1,2},{2,3},{3,4},{4,5},{5,6},{6,7},{7,8},{8,9},{9,10},{10,1... | collective-permute-start | bytes 98312 | tf_op jit(solution)/shard_map/ppermute | solution.py:14
  67.4 8.6 %collective-permute-start.11 = (bf16[2,16,4,128]{3,1,2,0:T(8,128)(2,1)S(1)}, bf16[2,16,4,128]{3,1,2,0:T(8,128)(2,1)S(1)}, u32[]{:S(2)}, u32[]{:S(2)}) collective-permute-start(bf16[2,16,4,128]{3,1,2,0:T(8,128)(2,1)S(1)} %copy.104), channel_id=1, source_target_pairs={{1,0},{2,1},{3,2},{4,3},{5,4},{6,5},{7,6},{8,7},{9,8},{10,9},{11,1... | collective-permute-start | bytes 98312 | tf_op jit(solution)/shard_map/ppermute | solution.py:17
  77.7 4.3 %collective-permute-start.12 = (bf16[2,16,4,128]{3,1,2,0:T(8,128)(2,1)S(1)}, bf16[2,16,4,128]{3,1,2,0:T(8,128)(2,1)S(1)}, u32[]{:S(2)}, u32[]{:S(2)}) collective-permute-start(bf16[2,16,4,128]{3,1,2,0:T(8,128)(2,1)S(1)} %fusion.46), channel_id=1, source_target_pairs={{0,1},{1,2},{2,3},{3,4},{4,5},{5,6},{6,7},{7,8},{8,9},{9,10},{10,1... | collective-permute-start | bytes 98312 | tf_op jit(solution)/shard_map/ppermute | solution.py:14
  79.6 8.6 %collective-permute-start.13 = (bf16[2,16,4,128]{3,1,2,0:T(8,128)(2,1)S(1)}, bf16[2,16,4,128]{3,1,2,0:T(8,128)(2,1)S(1)}, u32[]{:S(2)}, u32[]{:S(2)}) collective-permute-start(bf16[2,16,4,128]{3,1,2,0:T(8,128)(2,1)S(1)} %fusion.46), channel_id=1, source_target_pairs={{1,0},{2,1},{3,2},{4,3},{5,4},{6,5},{7,6},{8,7},{9,8},{10,9},{11,1... | collective-permute-start | bytes 98312 | tf_op jit(solution)/shard_map/ppermute | solution.py:17
  89.9 4.3 %collective-permute-start.14 = (bf16[2,16,4,128]{3,1,2,0:T(8,128)(2,1)S(1)}, bf16[2,16,4,128]{3,1,2,0:T(8,128)(2,1)S(1)}, u32[]{:S(2)}, u32[]{:S(2)}) collective-permute-start(bf16[2,16,4,128]{3,1,2,0:T(8,128)(2,1)S(1)} %fusion.47), channel_id=1, source_target_pairs={{0,1},{1,2},{2,3},{3,4},{4,5},{5,6},{6,7},{7,8},{8,9},{9,10},{10,1... | collective-permute-start | bytes 98312 | tf_op jit(solution)/shard_map/ppermute | solution.py:14
  91.8 8.6 %collective-permute-start.15 = (bf16[2,16,4,128]{3,1,2,0:T(8,128)(2,1)S(1)}, bf16[2,16,4,128]{3,1,2,0:T(8,128)(2,1)S(1)}, u32[]{:S(2)}, u32[]{:S(2)}) collective-permute-start(bf16[2,16,4,128]{3,1,2,0:T(8,128)(2,1)S(1)} %fusion.47), channel_id=1, source_target_pairs={{1,0},{2,1},{3,2},{4,3},{5,4},{6,5},{7,6},{8,7},{9,8},{10,9},{11,1... | collective-permute-start | bytes 98312 | tf_op jit(solution)/shard_map/ppermute | solution.py:17
  102.1 4.3 %collective-permute-start.16 = (bf16[2,16,4,128]{3,1,2,0:T(8,128)(2,1)S(1)}, bf16[2,16,4,128]{3,1,2,0:T(8,128)(2,1)S(1)}, u32[]{:S(2)}, u32[]{:S(2)}) collective-permute-start(bf16[2,16,4,128]{3,1,2,0:T(8,128)(2,1)S(1)} %fusion.48), channel_id=1, source_target_pairs={{0,1},{1,2},{2,3},{3,4},{4,5},{5,6},{6,7},{7,8},{8,9},{9,10},{10,1... | collective-permute-start | bytes 98312 | tf_op jit(solution)/shard_map/ppermute | solution.py:14
  104.0 8.6 %collective-permute-start.17 = (bf16[2,16,4,128]{3,1,2,0:T(8,128)(2,1)S(1)}, bf16[2,16,4,128]{3,1,2,0:T(8,128)(2,1)S(1)}, u32[]{:S(2)}, u32[]{:S(2)}) collective-permute-start(bf16[2,16,4,128]{3,1,2,0:T(8,128)(2,1)S(1)} %fusion.48), channel_id=1, source_target_pairs={{1,0},{2,1},{3,2},{4,3},{5,4},{6,5},{7,6},{8,7},{9,8},{10,9},{11,1... | collective-permute-start | bytes 98312 | tf_op jit(solution)/shard_map/ppermute | solution.py:17
  114.4 5.0 %collective-permute-start.18 = (f32[2,16,1,512]{3,1,2,0:T(8,128)S(1)}, f32[2,16,1,512]{3,1,2,0:T(8,128)S(1)}, u32[]{:S(2)}, u32[]{:S(2)}) collective-permute-start(f32[2,16,1,512]{3,1,2,0:T(8,128)S(1)} %pad_maximum_fusion.20), channel_id=1, source_target_pairs={{0,64},{64,128},{128,192},{1,65},{65,129},{129,193},{2,66},{66,130... | collective-permute-start | bytes 196616 | tf_op jit(solution)/shard_map/ppermute | solution.py:25
  119.4 5.0 %collective-permute-start.19 = (bf16[2,16,4,128]{3,1,2,0:T(8,128)(2,1)S(1)}, bf16[2,16,4,128]{3,1,2,0:T(8,128)(2,1)S(1)}, u32[]{:S(2)}, u32[]{:S(2)}) collective-permute-start(bf16[2,16,4,128]{3,1,2,0:T(8,128)(2,1)S(1)} %copy.116), channel_id=1, source_target_pairs={{0,1},{1,2},{2,3},{3,4},{4,5},{5,6},{6,7},{7,8},{8,9},{9,10},{10,1... | collective-permute-start | bytes 98312 | tf_op jit(solution)/shard_map/ppermute | solution.py:14
  122.5 8.6 %collective-permute-start.20 = (bf16[2,16,4,128]{3,1,2,0:T(8,128)(2,1)S(1)}, bf16[2,16,4,128]{3,1,2,0:T(8,128)(2,1)S(1)}, u32[]{:S(2)}, u32[]{:S(2)}) collective-permute-start(bf16[2,16,4,128]{3,1,2,0:T(8,128)(2,1)S(1)} %copy.116), channel_id=1, source_target_pairs={{1,0},{2,1},{3,2},{4,3},{5,4},{6,5},{7,6},{8,7},{9,8},{10,9},{11,1... | collective-permute-start | bytes 98312 | tf_op jit(solution)/shard_map/ppermute | solution.py:17
  132.5 12.0 %copy-start.1 = (f32[4,16,128]{2,1,0:T(8,128)}, f32[4,16,128]{2,1,0:T(8,128)S(1)}, u32[]{:S(2)}) copy-start(f32[4,16,128]{2,1,0:T(8,128)S(1)} %fusion.19) | copy-start | bytes 98308
  132.8 4.3 %collective-permute-start.21 = (bf16[2,16,4,128]{3,1,2,0:T(8,128)(2,1)S(1)}, bf16[2,16,4,128]{3,1,2,0:T(8,128)(2,1)S(1)}, u32[]{:S(2)}, u32[]{:S(2)}) collective-permute-start(bf16[2,16,4,128]{3,1,2,0:T(8,128)(2,1)S(1)} %fusion.49), channel_id=1, source_target_pairs={{0,1},{1,2},{2,3},{3,4},{4,5},{5,6},{6,7},{7,8},{8,9},{9,10},{10,1... | collective-permute-start | bytes 98312 | tf_op jit(solution)/shard_map/ppermute | solution.py:14
  134.7 8.6 %collective-permute-start.22 = (bf16[2,16,4,128]{3,1,2,0:T(8,128)(2,1)S(1)}, bf16[2,16,4,128]{3,1,2,0:T(8,128)(2,1)S(1)}, u32[]{:S(2)}, u32[]{:S(2)}) collective-permute-start(bf16[2,16,4,128]{3,1,2,0:T(8,128)(2,1)S(1)} %fusion.49), channel_id=1, source_target_pairs={{1,0},{2,1},{3,2},{4,3},{5,4},{6,5},{7,6},{8,7},{9,8},{10,9},{11,1... | collective-permute-start | bytes 98312 | tf_op jit(solution)/shard_map/ppermute | solution.py:17
  144.7 12.0 %copy-start.5 = (f32[4,16,128]{2,1,0:T(8,128)}, f32[4,16,128]{2,1,0:T(8,128)S(1)}, u32[]{:S(2)}) copy-start(f32[4,16,128]{2,1,0:T(8,128)S(1)} %fusion.17) | copy-start | bytes 98308
  145.0 12.0 %copy-start.3 = (f32[4,16,128]{2,1,0:T(8,128)}, f32[4,16,128]{2,1,0:T(8,128)S(1)}, u32[]{:S(2)}) copy-start(f32[4,16,128]{2,1,0:T(8,128)S(1)} %fusion.16) | copy-start | bytes 98308
  145.0 4.3 %collective-permute-start.23 = (bf16[2,16,4,128]{3,1,2,0:T(8,128)(2,1)S(1)}, bf16[2,16,4,128]{3,1,2,0:T(8,128)(2,1)S(1)}, u32[]{:S(2)}, u32[]{:S(2)}) collective-permute-start(bf16[2,16,4,128]{3,1,2,0:T(8,128)(2,1)S(1)} %fusion.50), channel_id=1, source_target_pairs={{0,1},{1,2},{2,3},{3,4},{4,5},{5,6},{6,7},{7,8},{8,9},{9,10},{10,1... | collective-permute-start | bytes 98312 | tf_op jit(solution)/shard_map/ppermute | solution.py:14
  146.9 8.6 %collective-permute-start.24 = (bf16[2,16,4,128]{3,1,2,0:T(8,128)(2,1)S(1)}, bf16[2,16,4,128]{3,1,2,0:T(8,128)(2,1)S(1)}, u32[]{:S(2)}, u32[]{:S(2)}) collective-permute-start(bf16[2,16,4,128]{3,1,2,0:T(8,128)(2,1)S(1)} %fusion.50), channel_id=1, source_target_pairs={{1,0},{2,1},{3,2},{4,3},{5,4},{6,5},{7,6},{8,7},{9,8},{10,9},{11,1... | collective-permute-start | bytes 98312 | tf_op jit(solution)/shard_map/ppermute | solution.py:17
  156.9 11.4 %copy-start.9 = (f32[4,16,128]{2,1,0:T(8,128)}, f32[4,16,128]{2,1,0:T(8,128)S(1)}, u32[]{:S(2)}) copy-start(f32[4,16,128]{2,1,0:T(8,128)S(1)} %fusion.15) | copy-start | bytes 98308
  157.2 11.2 %copy-start.7 = (f32[4,16,128]{2,1,0:T(8,128)}, f32[4,16,128]{2,1,0:T(8,128)S(1)}, u32[]{:S(2)}) copy-start(f32[4,16,128]{2,1,0:T(8,128)S(1)} %fusion.14) | copy-start | bytes 98308
  157.2 4.5 %collective-permute-start.25 = (bf16[2,16,4,128]{3,1,2,0:T(8,128)(2,1)S(1)}, bf16[2,16,4,128]{3,1,2,0:T(8,128)(2,1)S(1)}, u32[]{:S(2)}, u32[]{:S(2)}) collective-permute-start(bf16[2,16,4,128]{3,1,2,0:T(8,128)(2,1)S(1)} %fusion.51), channel_id=1, source_target_pairs={{0,1},{1,2},{2,3},{3,4},{4,5},{5,6},{6,7},{7,8},{8,9},{9,10},{10,1... | collective-permute-start | bytes 98312 | tf_op jit(solution)/shard_map/ppermute | solution.py:14
  159.1 8.6 %collective-permute-start.26 = (bf16[2,16,4,128]{3,1,2,0:T(8,128)(2,1)S(1)}, bf16[2,16,4,128]{3,1,2,0:T(8,128)(2,1)S(1)}, u32[]{:S(2)}, u32[]{:S(2)}) collective-permute-start(bf16[2,16,4,128]{3,1,2,0:T(8,128)(2,1)S(1)} %fusion.51), channel_id=1, source_target_pairs={{1,0},{2,1},{3,2},{4,3},{5,4},{6,5},{7,6},{8,7},{9,8},{10,9},{11,1... | collective-permute-start | bytes 98312 | tf_op jit(solution)/shard_map/ppermute | solution.py:17
  169.5 5.0 %collective-permute-start.27 = (f32[2,16,1,512]{3,1,2,0:T(8,128)S(1)}, f32[2,16,1,512]{3,1,2,0:T(8,128)S(1)}, u32[]{:S(2)}, u32[]{:S(2)}) collective-permute-start(f32[2,16,1,512]{3,1,2,0:T(8,128)S(1)} %pad_maximum_fusion.21), channel_id=1, source_target_pairs={{0,64},{64,128},{128,192},{1,65},{65,129},{129,193},{2,66},{66,130... | collective-permute-start | bytes 196616 | tf_op jit(solution)/shard_map/ppermute | solution.py:25
  174.6 5.0 %collective-permute-start.28 = (bf16[2,16,4,128]{3,1,2,0:T(8,128)(2,1)S(1)}, bf16[2,16,4,128]{3,1,2,0:T(8,128)(2,1)S(1)}, u32[]{:S(2)}, u32[]{:S(2)}) collective-permute-start(bf16[2,16,4,128]{3,1,2,0:T(8,128)(2,1)S(1)} %copy.128), channel_id=1, source_target_pairs={{0,1},{1,2},{2,3},{3,4},{4,5},{5,6},{6,7},{7,8},{8,9},{9,10},{10,1... | collective-permute-start | bytes 98312 | tf_op jit(solution)/shard_map/ppermute | solution.py:14
  177.7 8.6 %collective-permute-start.29 = (bf16[2,16,4,128]{3,1,2,0:T(8,128)(2,1)S(1)}, bf16[2,16,4,128]{3,1,2,0:T(8,128)(2,1)S(1)}, u32[]{:S(2)}, u32[]{:S(2)}) collective-permute-start(bf16[2,16,4,128]{3,1,2,0:T(8,128)(2,1)S(1)} %copy.128), channel_id=1, source_target_pairs={{1,0},{2,1},{3,2},{4,3},{5,4},{6,5},{7,6},{8,7},{9,8},{10,9},{11,1... | collective-permute-start | bytes 98312 | tf_op jit(solution)/shard_map/ppermute | solution.py:17
  187.9 4.3 %collective-permute-start.30 = (bf16[2,16,4,128]{3,1,2,0:T(8,128)(2,1)S(1)}, bf16[2,16,4,128]{3,1,2,0:T(8,128)(2,1)S(1)}, u32[]{:S(2)}, u32[]{:S(2)}) collective-permute-start(bf16[2,16,4,128]{3,1,2,0:T(8,128)(2,1)S(1)} %fusion.52), channel_id=1, source_target_pairs={{0,1},{1,2},{2,3},{3,4},{4,5},{5,6},{6,7},{7,8},{8,9},{9,10},{10,1... | collective-permute-start | bytes 98312 | tf_op jit(solution)/shard_map/ppermute | solution.py:14
  189.9 8.6 %collective-permute-start.31 = (bf16[2,16,4,128]{3,1,2,0:T(8,128)(2,1)S(1)}, bf16[2,16,4,128]{3,1,2,0:T(8,128)(2,1)S(1)}, u32[]{:S(2)}, u32[]{:S(2)}) collective-permute-start(bf16[2,16,4,128]{3,1,2,0:T(8,128)(2,1)S(1)} %fusion.52), channel_id=1, source_target_pairs={{1,0},{2,1},{3,2},{4,3},{5,4},{6,5},{7,6},{8,7},{9,8},{10,9},{11,1... | collective-permute-start | bytes 98312 | tf_op jit(solution)/shard_map/ppermute | solution.py:17
  200.1 4.3 %collective-permute-start.32 = (bf16[2,16,4,128]{3,1,2,0:T(8,128)(2,1)S(1)}, bf16[2,16,4,128]{3,1,2,0:T(8,128)(2,1)S(1)}, u32[]{:S(2)}, u32[]{:S(2)}) collective-permute-start(bf16[2,16,4,128]{3,1,2,0:T(8,128)(2,1)S(1)} %fusion.53), channel_id=1, source_target_pairs={{0,1},{1,2},{2,3},{3,4},{4,5},{5,6},{6,7},{7,8},{8,9},{9,10},{10,1... | collective-permute-start | bytes 98312 | tf_op jit(solution)/shard_map/ppermute | solution.py:14
  202.1 8.6 %collective-permute-start.33 = (bf16[2,16,4,128]{3,1,2,0:T(8,128)(2,1)S(1)}, bf16[2,16,4,128]{3,1,2,0:T(8,128)(2,1)S(1)}, u32[]{:S(2)}, u32[]{:S(2)}) collective-permute-start(bf16[2,16,4,128]{3,1,2,0:T(8,128)(2,1)S(1)} %fusion.53), channel_id=1, source_target_pairs={{1,0},{2,1},{3,2},{4,3},{5,4},{6,5},{7,6},{8,7},{9,8},{10,9},{11,1... | collective-permute-start | bytes 98312 | tf_op jit(solution)/shard_map/ppermute | solution.py:17
  211.8 5.6 %copy-start.2 = (f32[4,16,128]{2,1,0:T(8,128)S(1)}, f32[4,16,128]{2,1,0:T(8,128)}, u32[]{:S(2)}) copy-start(f32[4,16,128]{2,1,0:T(8,128)} %copy-done.1) | copy-start | bytes 98308
  212.4 9.8 %collective-permute-start.34 = (bf16[2,16,4,128]{3,1,2,0:T(8,128)(2,1)S(1)}, bf16[2,16,4,128]{3,1,2,0:T(8,128)(2,1)S(1)}, u32[]{:S(2)}, u32[]{:S(2)}) collective-permute-start(bf16[2,16,4,128]{3,1,2,0:T(8,128)(2,1)S(1)} %fusion.54), channel_id=1, source_target_pairs={{0,1},{1,2},{2,3},{3,4},{4,5},{5,6},{6,7},{7,8},{8,9},{9,10},{10,1... | collective-permute-start | bytes 98312 | tf_op jit(solution)/shard_map/ppermute | solution.py:14
  214.3 8.6 %collective-permute-start.35 = (bf16[2,16,4,128]{3,1,2,0:T(8,128)(2,1)S(1)}, bf16[2,16,4,128]{3,1,2,0:T(8,128)(2,1)S(1)}, u32[]{:S(2)}, u32[]{:S(2)}) collective-permute-start(bf16[2,16,4,128]{3,1,2,0:T(8,128)(2,1)S(1)} %fusion.54), channel_id=1, source_target_pairs={{1,0},{2,1},{3,2},{4,3},{5,4},{6,5},{7,6},{8,7},{9,8},{10,9},{11,1... | collective-permute-start | bytes 98312 | tf_op jit(solution)/shard_map/ppermute | solution.py:17
  224.3 18.0 %copy-start.18 = (f32[4,2,1,512]{3,2,1,0:T(1,128)S(1)}, f32[4,2,1,512]{3,2,1,0:T(1,128)}, u32[]{:S(2)}) copy-start(f32[4,2,1,512]{3,2,1,0:T(1,128)} %param.5) | copy-start | bytes 49156
  224.9 22.4 %copy-start = (f32[4,2,16,1,512]{4,3,2,1,0:T(1,128)S(1)}, f32[4,2,16,1,512]{4,3,2,1,0:T(1,128)}, u32[]{:S(2)}) copy-start(f32[4,2,16,1,512]{4,3,2,1,0:T(1,128)} %param.4) | copy-start | bytes 786436
  224.9 4.2 %collective-permute-start.36 = (f32[1,2,16,1,512]{4,2,3,1,0:T(8,128)S(1)}, f32[1,2,16,1,512]{4,2,3,1,0:T(8,128)S(1)}, u32[]{:S(2)}, u32[]{:S(2)}) collective-permute-start(f32[1,2,16,1,512]{4,2,3,1,0:T(8,128)S(1)} %get-tuple-element.9), channel_id=1, source_target_pairs={{64,0},{128,64},{192,128},{65,1},{129,65},{193,129},{66,2},{130,66... | collective-permute-start | bytes 196616 | tf_op jit(solution)/shard_map/ppermute | solution.py:17
  227.4 5.9 %collective-permute-start.37 = (f32[1,2,16,1,512]{4,2,3,1,0:T(8,128)S(1)}, f32[1,2,16,1,512]{4,2,3,1,0:T(8,128)S(1)}, u32[]{:S(2)}, u32[]{:S(2)}) collective-permute-start(f32[1,2,16,1,512]{4,2,3,1,0:T(8,128)S(1)} %get-tuple-element.8), channel_id=1, source_target_pairs={{0,64},{64,128},{128,192},{1,65},{65,129},{129,193},{2,66},{66,130... | collective-permute-start | bytes 196616 | tf_op jit(solution)/shard_map/ppermute | solution.py:14
  233.4 12.4 %collective-permute-start.38 = (f32[6,2,16,1,512]{4,2,3,1,0:T(8,128)S(1)}, f32[6,2,16,1,512]{4,2,3,1,0:T(8,128)S(1)}, u32[]{:S(2)}, u32[]{:S(2)}) collective-permute-start(f32[6,2,16,1,512]{4,2,3,1,0:T(8,128)S(1)} %pad_maximum_fusion), channel_id=1, source_target_pairs={{1,0},{2,1},{3,2},{4,3},{5,4},{6,5},{7,6},{8,7},{9,8},{10,9},{11,1... | collective-permute-start | bytes 1179656 | tf_op jit(solution)/shard_map/ppermute | solution.py:17
  235.8 11.2 %collective-permute-start.39 = (f32[6,2,16,1,512]{4,2,3,1,0:T(8,128)S(1)}, f32[6,2,16,1,512]{4,2,3,1,0:T(8,128)S(1)}, u32[]{:S(2)}, u32[]{:S(2)}) collective-permute-start(f32[6,2,16,1,512]{4,2,3,1,0:T(8,128)S(1)} %pad_maximum_fusion), channel_id=1, source_target_pairs={{0,1},{1,2},{2,3},{3,4},{4,5},{5,6},{6,7},{7,8},{8,9},{9,10},{10,1... | collective-permute-start | bytes 1179656 | tf_op jit(solution)/shard_map/ppermute | solution.py:14
  (11 other events, 28.5 us)
where the time goes:
time: 252 us; the launch traced here: 248 us
  waiting for transfers between devices  114 us (45%)
  starting transfers between devices  93.2 us (37%)
  local copies, waits for them, and re-layouts  20.6 us (8%)
  matrix products  16.2 us (6%)
    ppermute x18, waiting for transfers between devices, with_halo(): lax.ppermute(lax.slice_in_dim(block, 0, width, axis=dim), axis, backward)  95.7 us
    ppermute x18, starting transfers between devices, with_halo(): lax.ppermute(lax.slice_in_dim(block, block.shape[dim] - width, None, axis...  46.6 us
    ppermute x18, starting transfers between devices, with_halo(): lax.ppermute(lax.slice_in_dim(block, 0, width, axis=dim), axis, backward)  41.4 us
    dot_general x64, matrix products, product_of(): jnp.einsum(pattern, operand, matrix, preferred_element_type=jnp.float32)  16.2 us
    ppermute x4, waiting for transfers between devices, from_behind(): return lax.ppermute(block, axis, route)  13.1 us
    gather x32, local copies, waits for them, and re-layouts, apply_front(): picked = extended[:, :, where_from]  10.2 us
    ppermute x18, waiting for transfers between devices, with_halo(): lax.ppermute(lax.slice_in_dim(block, block.shape[dim] - width, None, axis...  5.46 us
    ppermute x4, starting transfers between devices, from_behind(): return lax.ppermute(block, axis, route)  5.17 us
  transfers between devices with their start and end apart: 40, of which 24 were waited for; matrix products, arithmetic and copies ran while one was open for 4% of the time, Pallas kernels for 0%

commit v1 on v0

v1 whole, which is shorter than its diff:
```python
import functools

import jax
import jax.numpy as jnp
from jax import lax
from jax.experimental import pallas as pl
from jax.experimental.pallas import tpu as pltpu
from jax.sharding import PartitionSpec as P

MESH = pl.DeviceIdType.MESH
F32, BF16 = jnp.float32, jnp.bfloat16
NB = 4
REMOTE = 5 * 128


def kernel(
    layers, tiles, src, shift, fro, col, sol, res,
    s_v, sh_v, fro_v, dense, ext, xo, xh, xlay, xs, acc, sol_v, res_v,
    lsem, lsend, lrecv, xsend, xrecv, csend, crecv, osem,
):
    l, t = lax.axis_index("layer"), lax.axis_index("tile")
    first, last = l == 0, l == layers - 1
    has_left, has_right = t > 0, t < tiles - 1

    barrier = pltpu.get_barrier_semaphore()
    for dl in (0, -1, 1):
        for dt in (-1, 0, 1):
            if dl == 0 and dt == 0:
                continue
            there = (l + dl >= 0) & (l + dl < layers) & (t + dt >= 0) & (t + dt < tiles)

            @pl.when(there)
            def _():
                pl.semaphore_signal(barrier, inc=1, device_id=(l + dl, t + dt), device_id_type=MESH)

    load_s = pltpu.make_async_copy(src, s_v.at[pl.ds(0, 4)], lsem.at[0])
    load_f = pltpu.make_async_copy(fro, fro_v, lsem.at[1])
    load_w = pltpu.make_async_copy(shift, sh_v, lsem.at[2])
    load_s.start()
    load_f.start()
    load_w.start()

    @pl.when(jnp.logical_not(has_left))
    def _():
        ext[:, 0:4] = jnp.zeros((5, 4, 32, 128), BF16)
        xh[:, 0] = jnp.zeros((4, 4, 32, 128), BF16)

    @pl.when(jnp.logical_not(has_right))
    def _():
        ext[:, 8:12] = jnp.zeros((5, 4, 32, 128), BF16)
        xh[:, 1] = jnp.zeros((4, 4, 32, 128), BF16)

    @pl.when(first)
    def _():
        xlay[0] = jnp.zeros((4, 32, 128), BF16)

    @pl.when(last)
    def _():
        xlay[1] = jnp.zeros((4, 32, 128), BF16)
        s_v[4] = jnp.zeros((2, 64, 128), F32)

    def source(q, part, b):
        return s_v[q, part, pl.ds(b, 16, stride=4), :]

    load_s.wait()

    @pl.when(first)
    def _():
        for b in range(NB):
            ext[0, 4 + b, 0:16] = source(0, 0, b).astype(BF16)
            ext[0, 4 + b, 16:32] = source(0, 1, b).astype(BF16)

    rows = jnp.where(first | last, 2, 3)
    cols = jnp.where(has_left & has_right, 3, 2)
    pl.semaphore_wait(barrier, rows * cols - 1)

    def load_copy(q, dt, to):
        return pltpu.make_async_remote_copy(
            src_ref=ext.at[q, pl.ds(4, 4)],
            dst_ref=ext.at[lax.rem(q, 4), pl.ds(4 - 4 * dt, 4)],
            send_sem=lsend.at[q, 1 + dt],
            recv_sem=lrecv.at[lax.rem(q, 4), 1 - dt],
            device_id=(to, t + dt),
            device_id_type=MESH,
        )

    def x_copy(q, dt):
        side = (1 - dt) // 2
        return pltpu.make_async_remote_copy(
            src_ref=xo.at[q],
            dst_ref=xh.at[q, side],
            send_sem=xsend.at[q, side],
            recv_sem=xrecv.at[q, side],
            device_id=(l, t + dt),
            device_id_type=MESH,
        )

    def layer_copy(dl):
        side = (1 - dl) // 2
        return pltpu.make_async_remote_copy(
            src_ref=xo.at[3 if dl == 1 else 0],
            dst_ref=xlay.at[side],
            send_sem=csend.at[side],
            recv_sem=crecv.at[side],
            device_id=(l + dl, t),
            device_id_type=MESH,
        )

    def source_copy():
        return pltpu.make_async_remote_copy(
            src_ref=s_v.at[0],
            dst_ref=s_v.at[4],
            send_sem=csend.at[2],
            recv_sem=crecv.at[2],
            device_id=(l - 1, t),
            device_id_type=MESH,
        )

    @pl.when(first & has_left)
    def _():
        load_copy(0, -1, l).start()

    @pl.when(first & has_right)
    def _():
        load_copy(0, 1, l).start()

    @pl.when(jnp.logical_not(first))
    def _():
        source_copy().start()

    load_f.wait()

    def densify(i, carry):
        b, r = i // 8, lax.rem(i, 8) * 16
        hit = [[col[b, k] == o for k in range(8)] for o in range(9)]
        for part in range(2):
            blocks = [fro_v[b, k, part, pl.ds(r, 16), :].astype(F32) for k in range(8)]
            for o in range(9):
                place = jnp.where(o < 4 - b, o, jnp.where(o >= 8 - b, o - 4, o + 1 + b))
                total = jnp.zeros((16, 128), F32)
                for k in range(8):
                    total = total + jnp.where(hit[o][k], blocks[k], 0.0)
                dense[b, pl.ds(pl.multiple_of(place * 128 + r, 16), 16), part * 128 : part * 128 + 128] = total.astype(BF16)
        return carry

    lax.fori_loop(0, 32, densify, 0)

    def plane(q, carry):
        @pl.when(jnp.logical_not(first) & (q == 0))
        def _():
            load_copy(0, 0, l).wait_recv()

        own = jnp.concatenate([ext[q, 4 + c] for c in range(4)], axis=1)
        for b in range(NB):
            acc[b] = jnp.dot(own, dense[b, REMOTE:], preferred_element_type=F32)

        @pl.when((q == 3) & jnp.logical_not(last))
        def _():
            source_copy().wait_recv()

        @pl.when(has_left)
        def _():
            load_copy(q, 1, l).wait_recv()

        @pl.when(has_right)
        def _():
            load_copy(q, -1, l).wait_recv()

        for b in range(NB):
            beside = [ext[q, c] for c in range(b, 4)] + [ext[q, 8 + c] for c in range(b + 1)]
            total = acc[b] + jnp.dot(
                jnp.concatenate(beside, axis=1), dense[b, 0:REMOTE], preferred_element_type=F32
            )
            re = total[0:16, 0:128] - total[16:32, 128:256]
            im = total[0:16, 128:256] + total[16:32, 0:128]
            ext[q + 1, 4 + b, 0:16] = (source(q + 1, 0, b) + re).astype(BF16)
            ext[q + 1, 4 + b, 16:32] = (source(q + 1, 1, b) + im).astype(BF16)
            xs[q + 1, 0, b] = re
            xs[q + 1, 1, b] = im

        onward = (q < 3) | jnp.logical_not(last)
        to = l + q // 3

        @pl.when(onward & has_left)
        def _():
            load_copy(q + 1, -1, to).start()

        @pl.when(onward & has_right)
        def _():
            load_copy(q + 1, 1, to).start()

        @pl.when((q == 3) & jnp.logical_not(last))
        def _():
            load_copy(q + 1, 0, to).start()

        for b in range(NB):
            for part in range(2):
                value = xs[q + 1, part, b]
                xo[q, b, part * 16 : part * 16 + 16] = value.astype(BF16)
                sol_v[q, part, pl.ds(b, 16, stride=4), :] = value

        @pl.when(has_left)
        def _():
            x_copy(q, -1).start()

        @pl.when(has_right)
        def _():
            x_copy(q, 1).start()

        @pl.when((q == 0) & jnp.logical_not(first))
        def _():
            layer_copy(-1).start()

        @pl.when((q == 3) & jnp.logical_not(last))
        def _():
            layer_copy(1).start()

        pltpu.make_async_copy(sol_v.at[q], sol.at[q], osem.at[0, q]).start()
        return carry

    lax.fori_loop(0, 4, plane, 0)

    load_w.wait()

    @pl.when(jnp.logical_not(first))
    def _():
        layer_copy(1).wait_recv()

    @pl.when(jnp.logical_not(last))
    def _():
        layer_copy(-1).wait_recv()

    for b in range(NB):
        for part in range(2):
            xs[0, part, b] = xlay[0, b, part * 16 : part * 16 + 16].astype(F32)
            xs[5, part, b] = xlay[1, b, part * 16 : part * 16 + 16].astype(F32)

    lane = lax.broadcasted_iota(jnp.int32, (16, 128), 1)

    def residual(q, carry):
        @pl.when(has_left)
        def _():
            x_copy(q, 1).wait_recv()

        @pl.when(has_right)
        def _():
            x_copy(q, -1).wait_recv()

        for b in range(NB):
            s_re = 6.0 - sh_v[q, pl.ds(b, 1), :]
            s_im = sh_v[q, pl.ds(4 + b, 1), :]
            x = [xs[q + 1, part, b] for part in range(2)]
            for part in range(2):
                up = pltpu.roll(x[part], 1, 1)
                before = pltpu.roll(xs[q + 1, part, b - 1], 1, 1) if b > 0 else jnp.zeros_like(up)
                down = pltpu.roll(x[part], 127, 1)
                after = pltpu.roll(xs[q + 1, part, b + 1], 127, 1) if b < 3 else jnp.zeros_like(up)
                beside = jnp.where(lane == 0, before, up) + jnp.where(lane == 127, after, down)
                beside = beside + xs[q, part, b] + xs[q + 2, part, b]
                half = slice(part * 16, part * 16 + 16)
                beside = beside + xh[q, 0, b, half].astype(F32) + xh[q, 1, b, half].astype(F32)
                cross = s_im * x[1] if part == 0 else -(s_im * x[0])
                value = s_re * x[part] + cross - beside
                res_v[q, part, pl.ds(b, 16, stride=4), :] = source(q, part, b) - value
        pltpu.make_async_copy(res_v.at[q], res.at[q], osem.at[1, q]).start()
        return carry

    lax.fori_loop(0, 4, residual, 0)

    @pl.when(first & has_left)
    def _():
        load_copy(0, -1, l).wait_send()

    @pl.when(first & has_right)
    def _():
        load_copy(0, 1, l).wait_send()

    @pl.when(jnp.logical_not(first))
    def _():
        source_copy().wait_send()
        layer_copy(-1).wait_send()

    @pl.when(jnp.logical_not(last))
    def _():
        load_copy(4, 0, l).wait_send()
        layer_copy(1).wait_send()

    def drain(q, carry):
        onward = (q < 3) | jnp.logical_not(last)

        @pl.when(has_left)
        def _():
            x_copy(q, -1).wait_send()

        @pl.when(has_right)
        def _():
            x_copy(q, 1).wait_send()

        @pl.when(onward & has_left)
        def _():
            load_copy(q + 1, -1, l).wait_send()

        @pl.when(onward & has_right)
        def _():
            load_copy(q + 1, 1, l).wait_send()

        pltpu.make_async_copy(sol_v.at[q], sol.at[q], osem.at[0, q]).wait()
        pltpu.make_async_copy(res_v.at[q], res.at[q], osem.at[1, q]).wait()
        return carry

    lax.fori_loop(0, 4, drain, 0)


def per_device(layers, tiles, source_field, wave_shift, frontal_blocks, block_columns):
    field = jax.ShapeDtypeStruct((4, 2, 64, 128), F32)
    hbm = pl.BlockSpec(memory_space=pl.ANY)
    dma = pltpu.SemaphoreType.DMA
    sol, res = pl.pallas_call(
        functools.partial(kernel, layers, tiles),
        out_shape=(field, field),
        in_specs=[hbm, hbm, hbm, pl.BlockSpec(memory_space=pltpu.SMEM)],
        out_specs=(hbm, hbm),
        scratch_shapes=[
            pltpu.VMEM((5, 2, 64, 128), F32),
            pltpu.VMEM((4, 8, 128), F32),
            pltpu.VMEM((4, 8, 2, 128, 128), BF16),
            pltpu.VMEM((4, 1152, 256), BF16),
            pltpu.VMEM((5, 12, 32, 128), BF16),
            pltpu.VMEM((4, 4, 32, 128), BF16),
            pltpu.VMEM((4, 2, 4, 32, 128), BF16),
            pltpu.VMEM((2, 4, 32, 128), BF16),
            pltpu.VMEM((6, 2, 4, 16, 128), F32),
            pltpu.VMEM((4, 32, 256), F32),
            pltpu.VMEM((4, 2, 64, 128), F32),
            pltpu.VMEM((4, 2, 64, 128), F32),
            dma((3,)),
            dma((5, 3)),
            dma((4, 3)),
            dma((4, 2)),
            dma((4, 2)),
            dma((3,)),
            dma((3,)),
            dma((2, 4)),
        ],
        compiler_params=pltpu.CompilerParams(
            collective_id=0, has_side_effects=True, vmem_limit_bytes=32 * 1024 * 1024
        ),
    )(
        source_field.reshape(4, 2, 64, 128),
        wave_shift.reshape(4, 8, 128),
        frontal_blocks[0],
        block_columns[0],
    )
    return sol.reshape(4, 2, 16, 1, 512), res.reshape(4, 2, 16, 1, 512)


def solution(mesh):
    placed = (
        P("layer", None, None, "tile", None),
        P("layer", None, "tile", None),
        P("layer", "tile", None, None, None, None),
        P("layer", "tile", None),
    )
    return jax.shard_map(
        functools.partial(per_device, mesh.shape["layer"], mesh.shape["tile"]),
        mesh=mesh,
        in_specs=placed,
        out_specs=(P("layer", None, None, "tile", None), P("layer", None, None, "tile", None)),
        check_vma=False,
    )
```

time: 252 us -> 87.8 us (0.35); the launches traced: 248 us -> 87.6 us
  waiting for transfers between devices: 114 us -> 0 us
  starting transfers between devices: 93.2 us -> 0 us
  Pallas kernels: 0 us -> 81.6 us
  matrix products: 16.2 us -> 0 us
  local copies, waits for them, and re-layouts: 20.6 us -> 5.34 us
    ppermute x40 -> x0, waiting for transfers between devices: 114 us -> none  [the longest x18 95.7 us: with_halo(): lax.ppermute(lax.slice_in_dim(block, 0, width, axis=dim), axis, backward)]
    ppermute x40 -> x0, starting transfers between devices: 93.2 us -> none  [the longest x18 46.6 us: with_halo(): lax.ppermute(lax.slice_in_dim(block, block.shape[dim] - width, None, axis...]
    pallas_call x0 -> x1, Pallas kernels: none -> 81.6 us  [per_device(): pl.pallas_call(functools.partial(kernel, layers, tiles), out_shape=(field...]
    dot_general x64 -> x0, matrix products: 16.2 us -> none  [product_of(): jnp.einsum(pattern, operand, matrix, preferred_element_type=jnp.float32)]
    gather x32 -> x0, local copies, waits for them, and re-layouts: 10.2 us -> none  [apply_front(): picked = extended[:, :, where_from]]
    another operation x38 -> x0, local copies, waits for them, and re-layouts: 4.86 us -> none  [apply_front(): return jnp.stack([real_part, imag_part]).reshape(vector.shape)]
    unnamed x42 -> x10, local copies, waits for them, and re-layouts: 3.77 us -> 5.34 us
  transfers between devices with their start and end apart: 40 -> 0, of which waited for: 24 -> 0; matrix products, arithmetic and copies ran while one was open for 4% -> 0% of each run, Pallas kernels for 0% -> 0%
where the time goes in v1:
time: 87.8 us; the launch traced here: 87.6 us
  Pallas kernels  81.6 us (93%)
  local copies, waits for them, and re-layouts  5.34 us (6%)
    pallas_call x1, Pallas kernels, per_device(): pl.pallas_call(functools.partial(kernel, layers, tiles), out_shape=(field...  81.6 us
    unnamed x10, local copies, waits for them, and re-layouts  5.34 us

profile of v1, /device:TPU:127, one launch (start us, length us, event | category | flops | bytes accessed | tf_op | source)
XLA Modules:
  0.0 87.6 jit_solution(9417896358273083424)
XLA Ops:
  0.6 0.0 copy-start
  0.6 1.6 %copy-done = bf16[1,4,8,2,128,128]{5,4,3,2,1,0:T(8,128)(2,1)S(1)} copy-done((bf16[1,4,8,2,128,128]{5,4,3,2,1,0:T(8,128)(2,1)S(1)}, bf16[1,4,8,2,128,128]{5,4,3,2,1,0:T(8,128)(2,1)}, u32[]{:S(2)}) %copy-start) | copy-done | bytes 2097176
  2.2 0.0 copy-start.1
  2.2 0.9 %copy-done.1 = f32[4,2,16,1,512]{4,3,2,1,0:T(1,128)S(1)} copy-done((f32[4,2,16,1,512]{4,3,2,1,0:T(1,128)S(1)}, f32[4,2,16,1,512]{4,3,2,1,0:T(1,128)}, u32[]{:S(2)}) %copy-start.1) | copy-done | bytes 262168
  3.2 0.0 copy-start.2
  3.2 0.7 copy-done.2
  3.9 0.0 copy-start.3
  3.9 0.7 copy-done.3
  4.6 81.6 %shard_map.59 = (f32[4,2,64,128]{3,2,1,0:T(8,128)S(1)}, f32[4,2,64,128]{3,2,1,0:T(8,128)S(1)}) custom-call(f32[4,2,64,128]{3,2,1,0:T(8,128)S(1)} %bitcast.9, f32[4,8,128]{2,1,0:T(8,128)S(1)} %bitcast.10, bf16[4,8,2,128,128]{4,3,2,1,0:T(8,128)(2,1)S(1)} %bitcast.6, s32[4,8]{1,0:T(4,128)S(1)} %bitcast.11), custom_call_target="tpu_custom_call" | custom-call | tf_op jit(solution)/shard_map/pallas_call | solution.py:318
  86.2 0.7 copy.10
  86.9 0.7 copy.11
Async XLA Ops:
  0.6 1.6 %copy-start = (bf16[1,4,8,2,128,128]{5,4,3,2,1,0:T(8,128)(2,1)S(1)}, bf16[1,4,8,2,128,128]{5,4,3,2,1,0:T(8,128)(2,1)}, u32[]{:S(2)}) copy-start(bf16[1,4,8,2,128,128]{5,4,3,2,1,0:T(8,128)(2,1)} %param.6) | copy-start | bytes 6291460
  2.2 0.9 %copy-start.1 = (f32[4,2,16,1,512]{4,3,2,1,0:T(1,128)S(1)}, f32[4,2,16,1,512]{4,3,2,1,0:T(1,128)}, u32[]{:S(2)}) copy-start(f32[4,2,16,1,512]{4,3,2,1,0:T(1,128)} %param.4) | copy-start | bytes 786436
  3.2 0.7 copy-start.2
  3.9 0.7 copy-start.3

commit v2 on v1

v2 whole, which is shorter than its diff:
```python
import functools

import jax
import jax.numpy as jnp
from jax import lax
from jax.experimental import pallas as pl
from jax.experimental.pallas import tpu as pltpu
from jax.sharding import PartitionSpec as P

MESH = pl.DeviceIdType.MESH
F32, BF16 = jnp.float32, jnp.bfloat16
NB = 4
TURN = 8
PAIRED = 2
FAR_LEFT, LEFT, OWN, RIGHT, FAR_RIGHT = 0, 4, 8, 12, 16
REMOTE = 5


def stages(b):
    return [
        ([3 - j] if 3 - j >= b else []) + ([8 + j] if j <= b else []) for j in range(4)
    ]


def places(b):
    return [c for stage in stages(b) for c in stage] + [4, 5, 6, 7]


def kernel(
    layers, tiles, src, shift, fro, columns, sol, res,
    s_v, sh_v, fro_v, col, dense, other, s_other, ext, xo, xh, xlay, xs, acc, sol_v, res_v,
    lsem, lsend, lrecv, fsend, frecv, xsend, xrecv, csend, crecv, gsend, grecv, osem,
):
    l, t = lax.axis_index("layer"), lax.axis_index("tile")
    first, last = l == 0, l == layers - 1
    has_left, has_right = t > 0, t < tiles - 1
    w = lax.rem(t, TURN)
    turn_left, turn_right = has_left & (w == 0), has_right & (w == TURN - 1)
    far_left = (t > 1) & (w <= 1)
    far_right = (t < tiles - 2) & (w >= TURN - 2)
    far = jnp.where(far_right, 2, -2)
    paired = l >= PAIRED

    barrier = pltpu.get_barrier_semaphore()
    for dl in (0, -1, 1):
        layer_there = (l + dl >= 0) & (l + dl < layers)
        for dt in (-1, 0, 1):
            if dl == 0 and dt == 0:
                continue
            there = layer_there & (t + dt >= 0) & (t + dt < tiles)

            @pl.when(there)
            def _():
                pl.semaphore_signal(barrier, inc=1, device_id=(l + dl, t + dt), device_id_type=MESH)

    for dl in (0, -1, 1):
        layer_there = (l + dl >= 0) & (l + dl < layers)

        @pl.when(layer_there & (far_left | far_right) & (l + max(dl, 0) >= PAIRED))
        def _():
            pl.semaphore_signal(barrier, inc=1, device_id=(l + dl, t + far), device_id_type=MESH)

    load_c = pltpu.make_async_copy(columns, col, lsem.at[0])
    load_s = pltpu.make_async_copy(src, s_v.at[pl.ds(0, 4)], lsem.at[1])
    load_w = pltpu.make_async_copy(shift, sh_v, lsem.at[2])
    load_f = [pltpu.make_async_copy(fro.at[b], fro_v.at[b], lsem.at[3 + b]) for b in range(NB)]
    load_c.start()
    load_f[0].start()
    load_s.start()
    for b in range(1, NB):
        load_f[b].start()
    load_w.start()

    @pl.when(jnp.logical_not(has_left))
    def _():
        ext[:, LEFT : LEFT + 4] = jnp.zeros((5, 4, 32, 128), BF16)
        xh[:, 0] = jnp.zeros((4, 4, 32, 128), BF16)

    @pl.when(jnp.logical_not(has_right))
    def _():
        ext[:, RIGHT : RIGHT + 4] = jnp.zeros((5, 4, 32, 128), BF16)
        xh[:, 1] = jnp.zeros((4, 4, 32, 128), BF16)

    @pl.when(first)
    def _():
        xlay[0] = jnp.zeros((4, 32, 128), BF16)

    @pl.when(last)
    def _():
        xlay[1] = jnp.zeros((4, 32, 128), BF16)
        s_v[4] = jnp.zeros((2, 64, 128), F32)

    def source(q, part, b):
        return s_v[q, part, pl.ds(b, 16, stride=4), :]

    load_c.wait()
    for b in range(NB):
        load_f[b].wait()
        hit = [[col[b, k] == c - b for k in range(8)] for c in places(b)]

        def densify(i, carry, b=b, hit=hit):
            r = pl.multiple_of(i * 16, 16)
            for part in range(2):
                blocks = [fro_v[b, k, part, pl.ds(r, 16), :].astype(F32) for k in range(8)]
                for place in range(9):
                    total = jnp.where(hit[place][0], blocks[0], 0.0)
                    for k in range(1, 8):
                        total = total + jnp.where(hit[place][k], blocks[k], 0.0)
                    dense[b, pl.ds(pl.multiple_of(place * 128 + r, 16), 16), part * 128 : part * 128 + 128] = total.astype(BF16)
            return carry

        lax.fori_loop(0, 8, densify, 0)

    load_s.wait()

    @pl.when(first)
    def _():
        for b in range(NB):
            ext[0, OWN + b, 0:16] = source(0, 0, b).astype(BF16)
            ext[0, OWN + b, 16:32] = source(0, 1, b).astype(BF16)

    rows = jnp.where(first | last, 2, 3)
    cols = jnp.where(has_left & has_right, 3, 2)
    far_rows = sum(
        jnp.where((l + dl >= 0) & (l + dl < layers) & (l + max(dl, 0) >= PAIRED), 1, 0) for dl in (0, -1, 1)
    )
    pl.semaphore_wait(barrier, rows * cols - 1 + jnp.where(far_left | far_right, far_rows, 0))

    def load_copy(q, dt, to, c):
        into = LEFT if dt == 1 else RIGHT
        return pltpu.make_async_remote_copy(
            src_ref=ext.at[q, OWN + c],
            dst_ref=ext.at[lax.rem(q, 4), into + c],
            send_sem=lsend.at[q, (1 + dt) // 2, c],
            recv_sem=lrecv.at[lax.rem(q, 4), (1 - dt) // 2, c],
            device_id=(to, t + dt),
            device_id_type=MESH,
        )

    def own_copy():
        return pltpu.make_async_remote_copy(
            src_ref=ext.at[4, pl.ds(OWN, 4)],
            dst_ref=ext.at[0, pl.ds(OWN, 4)],
            send_sem=csend.at[3],
            recv_sem=crecv.at[3],
            device_id=(l + 1, t),
            device_id_type=MESH,
        )

    def far_copy(q, dt, to):
        return pltpu.make_async_remote_copy(
            src_ref=ext.at[q, pl.ds(OWN, 4)],
            dst_ref=ext.at[lax.rem(q, 4), pl.ds(FAR_LEFT if dt == 2 else FAR_RIGHT, 4)],
            send_sem=fsend.at[q],
            recv_sem=frecv.at[lax.rem(q, 4)],
            device_id=(to, t + dt),
            device_id_type=MESH,
        )

    def x_copy(q, dt):
        side = (1 - dt) // 2
        return pltpu.make_async_remote_copy(
            src_ref=xo.at[q],
            dst_ref=xh.at[q, side],
            send_sem=xsend.at[q, side],
            recv_sem=xrecv.at[q, side],
            device_id=(l, t + dt),
            device_id_type=MESH,
        )

    def layer_copy(dl):
        side = (1 - dl) // 2
        return pltpu.make_async_remote_copy(
            src_ref=xo.at[3 if dl == 1 else 0],
            dst_ref=xlay.at[side],
            send_sem=csend.at[side],
            recv_sem=crecv.at[side],
            device_id=(l + dl, t),
            device_id_type=MESH,
        )

    def source_copy():
        return pltpu.make_async_remote_copy(
            src_ref=s_v.at[0],
            dst_ref=s_v.at[4],
            send_sem=csend.at[2],
            recv_sem=crecv.at[2],
            device_id=(l - 1, t),
            device_id_type=MESH,
        )

    across = t + jnp.where(turn_left, -1, 1)

    def turn_copies():
        pieces = [(dense, other), (s_v.at[1], s_other.at[0]), (s_v.at[3], s_other.at[1])]
        return [
            pltpu.make_async_remote_copy(
                src_ref=here,
                dst_ref=there,
                send_sem=gsend.at[i],
                recv_sem=grecv.at[i],
                device_id=(l, across),
                device_id_type=MESH,
            )
            for i, (here, there) in enumerate(pieces)
        ]

    at_turn = paired & (turn_left | turn_right)

    def sends_load(q, dt):
        there = has_left if dt == -1 else has_right
        turn = turn_left if dt == -1 else turn_right
        return there & jnp.logical_not(paired & turn & (lax.rem(q, 2) == 1))

    for step in range(4):
        @pl.when(first & has_left)
        def _():
            load_copy(0, -1, l, step).start()

        @pl.when(first & has_right)
        def _():
            load_copy(0, 1, l, 3 - step).start()

    @pl.when(jnp.logical_not(first))
    def _():
        source_copy().start()

    @pl.when(at_turn)
    def _():
        for copy in turn_copies()[::-1]:
            copy.start()

    def product(q, window, matrix, b, start, blocks):
        operand = jnp.concatenate([ext[q, window + c] for c in blocks], axis=1)
        return jnp.dot(
            operand,
            matrix[b, start * 128 : (start + len(blocks)) * 128],
            preferred_element_type=F32,
        )

    def combine(total):
        re = total[0:16, 0:128] - total[16:32, 128:256]
        im = total[0:16, 128:256] + total[16:32, 0:128]
        return re, im

    def plane(q, carry):
        @pl.when(jnp.logical_not(first) & (q == 0))
        def _():
            own_copy().wait_recv()

        for b in range(NB):
            acc[b] = product(q, LEFT, dense, b, REMOTE, [4, 5, 6, 7])

        @pl.when((q == 3) & jnp.logical_not(last))
        def _():
            source_copy().wait_recv()

        for j in range(4):
            @pl.when(sends_load(q, -1))
            def _():
                load_copy(q, 1, l, 3 - j).wait_recv()

            @pl.when(sends_load(q, 1))
            def _():
                load_copy(q, -1, l, j).wait_recv()

            for b in range(NB):
                needs = stages(b)[j]
                if not needs:
                    continue
                start = sum(len(s) for s in stages(b)[:j])
                total = acc[b] + product(q, LEFT, dense, b, start, needs)
                if any(stages(b)[j + 1 :]):
                    acc[b] = total
                    continue
                re, im = combine(total)
                ext[q + 1, OWN + b, 0:16] = (source(q + 1, 0, b) + re).astype(BF16)
                ext[q + 1, OWN + b, 16:32] = (source(q + 1, 1, b) + im).astype(BF16)
                xs[q + 1, 0, b] = re
                xs[q + 1, 1, b] = im

        handing = (q == 3) & jnp.logical_not(last)
        onward = (q < 3) | jnp.logical_not(last)
        to = l + q // 3

        for step in range(4):
            @pl.when(onward & (handing & has_left | (q < 3) & sends_load(q + 1, -1)))
            def _():
                load_copy(q + 1, -1, to, step).start()

            @pl.when(onward & (handing & has_right | (q < 3) & sends_load(q + 1, 1)))
            def _():
                load_copy(q + 1, 1, to, 3 - step).start()

        @pl.when(handing)
        def _():
            own_copy().start()

        sends_far = (handing & (l + 1 >= PAIRED)) | ((q == 1) & paired)

        @pl.when(sends_far & far_left & (w == 1))
        def _():
            far_copy(q + 1, -2, to).start()

        @pl.when(sends_far & far_right & (w == TURN - 2))
        def _():
            far_copy(q + 1, 2, to).start()

        @pl.when(at_turn & (lax.rem(q, 2) == 0))
        def _():
            @pl.when(q == 0)
            def _():
                for copy in turn_copies():
                    copy.wait_recv()

            window = jnp.where(turn_left, FAR_LEFT, OWN)
            into = jnp.where(turn_left, LEFT, RIGHT)
            for b in range(NB):
                acc[b] = product(q, window, other, b, REMOTE, [4, 5, 6, 7])

            @pl.when(turn_left)
            def _():
                far_copy(q, 2, l).wait_recv()

            @pl.when(turn_right)
            def _():
                far_copy(q, -2, l).wait_recv()

            for b in range(NB):
                total = acc[b] + product(q, window, other, b, 0, places(b)[:REMOTE])
                re, im = combine(total)
                there = [s_other[q // 2, part, pl.ds(b, 16, stride=4), :] for part in range(2)]
                ext[q + 1, into + b, 0:16] = (there[0] + re).astype(BF16)
                ext[q + 1, into + b, 16:32] = (there[1] + im).astype(BF16)

        for b in range(NB):
            for part in range(2):
                value = xs[q + 1, part, b]
                xo[q, b, part * 16 : part * 16 + 16] = value.astype(BF16)
                sol_v[q, part, pl.ds(b, 16, stride=4), :] = value

        @pl.when(has_left)
        def _():
            x_copy(q, -1).start()

        @pl.when(has_right)
        def _():
            x_copy(q, 1).start()

        @pl.when((q == 0) & jnp.logical_not(first))
        def _():
            layer_copy(-1).start()

        @pl.when(handing)
        def _():
            layer_copy(1).start()

        pltpu.make_async_copy(sol_v.at[q], sol.at[q], osem.at[0, q]).start()
        return carry

    lax.fori_loop(0, 4, plane, 0)

    load_w.wait()

    @pl.when(jnp.logical_not(first))
    def _():
        layer_copy(1).wait_recv()

    @pl.when(jnp.logical_not(last))
    def _():
        layer_copy(-1).wait_recv()

    for b in range(NB):
        for part in range(2):
            xs[0, part, b] = xlay[0, b, part * 16 : part * 16 + 16].astype(F32)
            xs[5, part, b] = xlay[1, b, part * 16 : part * 16 + 16].astype(F32)

    lane = lax.broadcasted_iota(jnp.int32, (16, 128), 1)

    def residual(q, carry):
        @pl.when(has_left)
        def _():
            x_copy(q, 1).wait_recv()

        @pl.when(has_right)
        def _():
            x_copy(q, -1).wait_recv()

        for b in range(NB):
            s_re = 6.0 - sh_v[q, pl.ds(b, 1), :]
            s_im = sh_v[q, pl.ds(4 + b, 1), :]
            x = [xs[q + 1, part, b] for part in range(2)]
            for part in range(2):
                up = pltpu.roll(x[part], 1, 1)
                before = pltpu.roll(xs[q + 1, part, b - 1], 1, 1) if b > 0 else jnp.zeros_like(up)
                down = pltpu.roll(x[part], 127, 1)
                after = pltpu.roll(xs[q + 1, part, b + 1], 127, 1) if b < 3 else jnp.zeros_like(up)
                beside = jnp.where(lane == 0, before, up) + jnp.where(lane == 127, after, down)
                beside = beside + xs[q, part, b] + xs[q + 2, part, b]
                half = slice(part * 16, part * 16 + 16)
                beside = beside + xh[q, 0, b, half].astype(F32) + xh[q, 1, b, half].astype(F32)
                cross = s_im * x[1] if part == 0 else -(s_im * x[0])
                value = s_re * x[part] + cross - beside
                res_v[q, part, pl.ds(b, 16, stride=4), :] = source(q, part, b) - value
        pltpu.make_async_copy(res_v.at[q], res.at[q], osem.at[1, q]).start()
        return carry

    lax.fori_loop(0, 4, residual, 0)

    for c in range(4):
        @pl.when(first & has_left)
        def _():
            load_copy(0, -1, l, c).wait_send()

        @pl.when(first & has_right)
        def _():
            load_copy(0, 1, l, c).wait_send()

    @pl.when(jnp.logical_not(first))
    def _():
        source_copy().wait_send()
        layer_copy(-1).wait_send()

    @pl.when(jnp.logical_not(last))
    def _():
        own_copy().wait_send()
        layer_copy(1).wait_send()

    @pl.when(at_turn)
    def _():
        for copy in turn_copies():
            copy.wait_send()

    @pl.when(paired & (far_left & (w == 1) | far_right & (w == TURN - 2)))
    def _():
        far_copy(2, 2, l).wait_send()

    @pl.when(jnp.logical_not(last) & (l + 1 >= PAIRED) & (far_left & (w == 1) | far_right & (w == TURN - 2)))
    def _():
        far_copy(4, 2, l).wait_send()

    def drain(q, carry):
        @pl.when(has_left)
        def _():
            x_copy(q, -1).wait_send()

        @pl.when(has_right)
        def _():
            x_copy(q, 1).wait_send()

        handing = (q == 3) & jnp.logical_not(last)
        for c in range(4):
            @pl.when(handing & has_left | (q < 3) & sends_load(q + 1, -1))
            def _():
                load_copy(q + 1, -1, l, c).wait_send()

            @pl.when(handing & has_right | (q < 3) & sends_load(q + 1, 1))
            def _():
                load_copy(q + 1, 1, l, c).wait_send()

        pltpu.make_async_copy(sol_v.at[q], sol.at[q], osem.at[0, q]).wait()
        pltpu.make_async_copy(res_v.at[q], res.at[q], osem.at[1, q]).wait()
        return carry

    lax.fori_loop(0, 4, drain, 0)


def per_device(layers, tiles, source_field, wave_shift, frontal_blocks, block_columns):
    field = jax.ShapeDtypeStruct((4, 2, 64, 128), F32)
    hbm = pl.BlockSpec(memory_space=pltpu.HBM)
    anywhere = pl.BlockSpec(memory_space=pl.ANY)
    dma = pltpu.SemaphoreType.DMA
    sol, res = pl.pallas_call(
        functools.partial(kernel, layers, tiles),
        out_shape=(field, field),
        in_specs=[hbm, hbm, hbm, hbm],
        out_specs=(anywhere, anywhere),
        scratch_shapes=[
            pltpu.VMEM((5, 2, 64, 128), F32),
            pltpu.VMEM((4, 8, 128), F32),
            pltpu.VMEM((4, 8, 2, 128, 128), BF16),
            pltpu.SMEM((4, 8), jnp.int32),
            pltpu.VMEM((4, 1152, 256), BF16),
            pltpu.VMEM((4, 1152, 256), BF16),
            pltpu.VMEM((2, 2, 64, 128), F32),
            pltpu.VMEM((5, 20, 32, 128), BF16),
            pltpu.VMEM((4, 4, 32, 128), BF16),
            pltpu.VMEM((4, 2, 4, 32, 128), BF16),
            pltpu.VMEM((2, 4, 32, 128), BF16),
            pltpu.VMEM((6, 2, 4, 16, 128), F32),
            pltpu.VMEM((4, 32, 256), F32),
            pltpu.VMEM((4, 2, 64, 128), F32),
            pltpu.VMEM((4, 2, 64, 128), F32),
            dma((7,)),
            dma((5, 2, 4)),
            dma((4, 2, 4)),
            dma((5,)),
            dma((4,)),
            dma((4, 2)),
            dma((4, 2)),
            dma((4,)),
            dma((4,)),
            dma((3,)),
            dma((3,)),
            dma((2, 4)),
        ],
        compiler_params=pltpu.CompilerParams(
            collective_id=0, has_side_effects=True, vmem_limit_bytes=60 * 1024 * 1024
        ),
    )(
        source_field.reshape(4, 2, 64, 128),
        wave_shift.reshape(4, 8, 128),
        frontal_blocks[0],
        block_columns[0],
    )
    return sol.reshape(4, 2, 16, 1, 512), res.reshape(4, 2, 16, 1, 512)


def solution(mesh):
    placed = (
        P("layer", None, None, "tile", None),
        P("layer", None, "tile", None),
        P("layer", "tile", None, None, None, None),
        P("layer", "tile", None),
    )
    return jax.shard_map(
        functools.partial(per_device, mesh.shape["layer"], mesh.shape["tile"]),
        mesh=mesh,
        in_specs=placed,
        out_specs=(P("layer", None, None, "tile", None), P("layer", None, None, "tile", None)),
        check_vma=False,
    )
```

time: 87.8 us -> 77.5 us (0.88)
  Pallas kernels: 81.6 us -> 73.4 us
  local copies, waits for them, and re-layouts: 5.34 us -> 3.34 us
    pallas_call x1, Pallas kernels: 81.6 us -> 73.4 us  [per_device(): pl.pallas_call(functools.partial(kernel, layers, tiles), out_shape=(field...]
    unnamed x10 -> x2, local copies, waits for them, and re-layouts: 5.34 us -> 3.34 us
where the time goes in v2:
time: 77.5 us; the launch traced here: 77.4 us
  Pallas kernels  73.4 us (95%)
  local copies, waits for them, and re-layouts  3.34 us (4%)
    pallas_call x1, Pallas kernels, per_device(): pl.pallas_call(functools.partial(kernel, layers, tiles), out_shape=(field...  73.4 us
    unnamed x2, local copies, waits for them, and re-layouts  3.34 us

profile of v2, /device:TPU:127, one launch (start us, length us, event | category | flops | bytes accessed | tf_op | source)
XLA Modules:
  0.0 77.4 jit_solution(3161376177430268949)
XLA Ops:
  0.6 73.4 %shard_map.59 = (f32[4,2,64,128]{3,2,1,0:T(8,128)}, f32[4,2,64,128]{3,2,1,0:T(8,128)}) custom-call(f32[4,2,64,128]{3,2,1,0:T(8,128)} %bitcast.9, f32[4,8,128]{2,1,0:T(8,128)} %bitcast.10, bf16[4,8,2,128,128]{4,3,2,1,0:T(8,128)(2,1)} %bitcast.6, s32[4,8]{1,0:T(4,128)} %bitcast.11), custom_call_target="tpu_custom_call" | custom-call | tf_op jit(solution)/shard_map/pallas_call | solution.py:473
  74.0 1.7 %copy.10 = f32[4,2,16,1,512]{4,3,2,1,0:T(1,128)} copy(f32[4,2,16,1,512]{4,3,2,1,0:T(1,128)} %bitcast.8) | data formatting | bytes 524288
  75.7 1.7 %copy.11 = f32[4,2,16,1,512]{4,3,2,1,0:T(1,128)} copy(f32[4,2,16,1,512]{4,3,2,1,0:T(1,128)} %bitcast.7) | data formatting | bytes 524288

commit v3 on v2

--- a/solution.py
+++ b/solution.py
@@ -13,12 +13,16 @@
 TURN = 8
 PAIRED = 2
 FAR_LEFT, LEFT, OWN, RIGHT, FAR_RIGHT = 0, 4, 8, 12, 16
+CUTS = 2
+PIECE = NB // CUTS
 REMOTE = 5
 
 
 def stages(b):
     return [
-        ([3 - j] if 3 - j >= b else []) + ([8 + j] if j <= b else []) for j in range(4)
+        [c for c in range(4 - PIECE * (j + 1), 4 - PIECE * j) if c >= b]
+        + [8 + c for c in range(PIECE * j, PIECE * (j + 1)) if c <= b]
+        for j in range(CUTS)
     ]
 
 
@@ -126,13 +130,14 @@
     )
     pl.semaphore_wait(barrier, rows * cols - 1 + jnp.where(far_left | far_right, far_rows, 0))
 
-    def load_copy(q, dt, to, c):
+    def load_copy(q, dt, to, j):
         into = LEFT if dt == 1 else RIGHT
+        c = 4 - PIECE * (j + 1) if dt == 1 else PIECE * j
         return pltpu.make_async_remote_copy(
-            src_ref=ext.at[q, OWN + c],
-            dst_ref=ext.at[lax.rem(q, 4), into + c],
-            send_sem=lsend.at[q, (1 + dt) // 2, c],
-            recv_sem=lrecv.at[lax.rem(q, 4), (1 - dt) // 2, c],
+            src_ref=ext.at[q, pl.ds(OWN + c, PIECE)],
+            dst_ref=ext.at[lax.rem(q, 4), pl.ds(into + c, PIECE)],
+            send_sem=lsend.at[q, (1 + dt) // 2, j],
+            recv_sem=lrecv.at[lax.rem(q, 4), (1 - dt) // 2, j],
             device_id=(to, t + dt),
             device_id_type=MESH,
         )
@@ -212,14 +217,14 @@
         turn = turn_left if dt == -1 else turn_right
         return there & jnp.logical_not(paired & turn & (lax.rem(q, 2) == 1))
 
-    for step in range(4):
+    for step in range(CUTS):
         @pl.when(first & has_left)
         def _():
             load_copy(0, -1, l, step).start()
 
         @pl.when(first & has_right)
         def _():
-            load_copy(0, 1, l, 3 - step).start()
+            load_copy(0, 1, l, step).start()
 
     @pl.when(jnp.logical_not(first))
     def _():
@@ -243,6 +248,32 @@
         im = total[0:16, 128:256] + total[16:32, 0:128]
         return re, im
 
+    def publish(q):
+        for b in range(NB):
+            for part in range(2):
+                xo[q, b, part * 16 : part * 16 + 16] = xs[q + 1, part, b].astype(BF16)
+
+        @pl.when(has_left)
+        def _():
+            x_copy(q, -1).start()
+
+        @pl.when(has_right)
+        def _():
+            x_copy(q, 1).start()
+
+        @pl.when((q == 0) & jnp.logical_not(first))
+        def _():
+            layer_copy(-1).start()
+
+        @pl.when((q == 3) & jnp.logical_not(last))
+        def _():
+            layer_copy(1).start()
+
+        for b in range(NB):
+            for part in range(2):
+                sol_v[q, part, pl.ds(b, 16, stride=4), :] = xs[q + 1, part, b]
+        pltpu.make_async_copy(sol_v.at[q], sol.at[q], osem.at[0, q]).start()
+
     def plane(q, carry):
         @pl.when(jnp.logical_not(first) & (q == 0))
         def _():
@@ -255,10 +286,10 @@
         def _():
             source_copy().wait_recv()
 
-        for j in range(4):
+        for j in range(CUTS):
             @pl.when(sends_load(q, -1))
             def _():
-                load_copy(q, 1, l, 3 - j).wait_recv()
+                load_copy(q, 1, l, j).wait_recv()
 
             @pl.when(sends_load(q, 1))
             def _():
@@ -283,14 +314,14 @@
         onward = (q < 3) | jnp.logical_not(last)
         to = l + q // 3
 
-        for step in range(4):
+        for step in range(CUTS):
             @pl.when(onward & (handing & has_left | (q < 3) & sends_load(q + 1, -1)))
             def _():
                 load_copy(q + 1, -1, to, step).start()
 
             @pl.when(onward & (handing & has_right | (q < 3) & sends_load(q + 1, 1)))
             def _():
-                load_copy(q + 1, 1, to, 3 - step).start()
+                load_copy(q + 1, 1, to, step).start()
 
         @pl.when(handing)
         def _():
@@ -333,29 +364,11 @@
                 ext[q + 1, into + b, 0:16] = (there[0] + re).astype(BF16)
                 ext[q + 1, into + b, 16:32] = (there[1] + im).astype(BF16)
 
-        for b in range(NB):
-            for part in range(2):
-                value = xs[q + 1, part, b]
-                xo[q, b, part * 16 : part * 16 + 16] = value.astype(BF16)
-                sol_v[q, part, pl.ds(b, 16, stride=4), :] = value
-
-        @pl.when(has_left)
-        def _():
-            x_copy(q, -1).start()
-
-        @pl.when(has_right)
-        def _():
-            x_copy(q, 1).start()
-
-        @pl.when((q == 0) & jnp.logical_not(first))
-        def _():
-            layer_copy(-1).start()
-
-        @pl.when(handing)
-        def _():
-            layer_copy(1).start()
-
-        pltpu.make_async_copy(sol_v.at[q], sol.at[q], osem.at[0, q]).start()
+        @pl.when(lax.rem(q, 2) == 1)
+        def _():
+            publish(q)
+            publish(q - 1)
+
         return carry
 
     lax.fori_loop(0, 4, plane, 0)
@@ -407,7 +420,7 @@
 
     lax.fori_loop(0, 4, residual, 0)
 
-    for c in range(4):
+    for c in range(CUTS):
         @pl.when(first & has_left)
         def _():
             load_copy(0, -1, l, c).wait_send()
@@ -449,7 +462,7 @@
             x_copy(q, 1).wait_send()
 
         handing = (q == 3) & jnp.logical_not(last)
-        for c in range(4):
+        for c in range(CUTS):
             @pl.when(handing & has_left | (q < 3) & sends_load(q + 1, -1))
             def _():
                 load_copy(q + 1, -1, l, c).wait_send()
@@ -492,8 +505,8 @@
             pltpu.VMEM((4, 2, 64, 128), F32),
             pltpu.VMEM((4, 2, 64, 128), F32),
             dma((7,)),
-            dma((5, 2, 4)),
-            dma((4, 2, 4)),
+            dma((5, 2, CUTS)),
+            dma((4, 2, CUTS)),
             dma((5,)),
             dma((4,)),
             dma((4, 2)),
@@ -505,13 +518,18 @@
             dma((2, 4)),
         ],
         compiler_params=pltpu.CompilerParams(
-            collective_id=0, has_side_effects=True, vmem_limit_bytes=60 * 1024 * 1024
+            collective_id=0, has_side_effects=True, vmem_limit_bytes=32 * 1024 * 1024
         ),
     )(
-        source_field.reshape(4, 2, 64, 128),
-        wave_shift.reshape(4, 8, 128),
-        frontal_blocks[0],
-        block_columns[0],
+        *[
+            pltpu.with_memory_space_constraint(operand, pltpu.HBM)
+            for operand in (
+                source_field.reshape(4, 2, 64, 128),
+                wave_shift.reshape(4, 8, 128),
+                frontal_blocks[0],
+                block_columns[0],
+            )
+        ]
     )
     return sol.reshape(4, 2, 16, 1, 512), res.reshape(4, 2, 16, 1, 512)
 

time: 77.5 us -> 74.1 us (0.956)
  local copies, waits for them, and re-layouts: 3.34 us -> 1.41 us
  Pallas kernels: 73.4 us -> 72 us
    unnamed x2, local copies, waits for them, and re-layouts: 3.34 us -> 1.41 us
    pallas_call x1, Pallas kernels: 73.4 us -> 72 us  [per_device(): pl.pallas_call(functools.partial(kernel, layers, tiles), out_shape=(field...]
where the time goes in v3:
time: 74.1 us; the launch traced here: 74 us
  Pallas kernels  72 us (97%)
  local copies, waits for them, and re-layouts  1.41 us (2%)
    pallas_call x1, Pallas kernels, per_device(): pl.pallas_call(functools.partial(kernel, layers, tiles), out_shape=(field...  72 us

profile of v3, /device:TPU:127, one launch (start us, length us, event | category | flops | bytes accessed | tf_op | source)
XLA Modules:
  0.0 74.0 jit_solution(3155273104728214922)
XLA Ops:
  0.6 72.0 %shard_map.59 = (f32[4,2,64,128]{3,2,1,0:T(8,128)S(1)}, f32[4,2,64,128]{3,2,1,0:T(8,128)S(1)}) custom-call(f32[4,2,64,128]{3,2,1,0:T(8,128)} %bitcast.9, f32[4,8,128]{2,1,0:T(8,128)} %bitcast.10, bf16[4,8,2,128,128]{4,3,2,1,0:T(8,128)(2,1)} %bitcast.8, s32[4,8]{1,0:T(4,128)} %bitcast.11), custom_call_target="tpu_custom_call" | custom-call | tf_op jit(solution)/shard_map/pallas_call | solution.py:486
  72.6 0.7 copy.10
  73.3 0.7 copy.11

commit v4 on v3

--- a/solution.py
+++ b/solution.py
@@ -11,7 +11,10 @@
 F32, BF16 = jnp.float32, jnp.bfloat16
 NB = 4
 TURN = 8
-PAIRED = 2
+PAIRED = 1
+ROUTE = {7: (-2, -3), 4: (3, 6), 2: (-6, -2), 0: (2, 3), 3: (-3, -6), 5: (6, 2)}
+ROUTED = 5
+SPAN = 288
 FAR_LEFT, LEFT, OWN, RIGHT, FAR_RIGHT = 0, 4, 8, 12, 16
 CUTS = 2
 PIECE = NB // CUTS
@@ -33,7 +36,7 @@
 def kernel(
     layers, tiles, src, shift, fro, columns, sol, res,
     s_v, sh_v, fro_v, col, dense, other, s_other, ext, xo, xh, xlay, xs, acc, sol_v, res_v,
-    lsem, lsend, lrecv, fsend, frecv, xsend, xrecv, csend, crecv, gsend, grecv, osem,
+    lsem, lsend, lrecv, fsend, frecv, xsend, xrecv, csend, crecv, gsend, grecv, rsend, rrecv, osem,
 ):
     l, t = lax.axis_index("layer"), lax.axis_index("tile")
     first, last = l == 0, l == layers - 1
@@ -44,6 +47,10 @@
     far_right = (t < tiles - 2) & (w >= TURN - 2)
     far = jnp.where(far_right, 2, -2)
     paired = l >= PAIRED
+    onto_next = (w == 7) | (w == 4) | (w == 5)
+    on_route = paired & ((onto_next & (t < tiles - TURN)) | (((w == 0) | (w == 2) | (w == 3)) & (t >= TURN)))
+    route_from = t + sum(jnp.where(w == place, ROUTE[place][0], 0) for place in ROUTE)
+    route_to = t + sum(jnp.where(w == place, ROUTE[place][1], 0) for place in ROUTE)
 
     barrier = pltpu.get_barrier_semaphore()
     for dl in (0, -1, 1):
@@ -63,6 +70,11 @@
         @pl.when(layer_there & (far_left | far_right) & (l + max(dl, 0) >= PAIRED))
         def _():
             pl.semaphore_signal(barrier, inc=1, device_id=(l + dl, t + far), device_id_type=MESH)
+
+    @pl.when(on_route)
+    def _():
+        for there in (route_from, route_to):
+            pl.semaphore_signal(barrier, inc=1, device_id=(l, there), device_id_type=MESH)
 
     load_c = pltpu.make_async_copy(columns, col, lsem.at[0])
     load_s = pltpu.make_async_copy(src, s_v.at[pl.ds(0, 4)], lsem.at[1])
@@ -128,7 +140,7 @@
     far_rows = sum(
         jnp.where((l + dl >= 0) & (l + dl < layers) & (l + max(dl, 0) >= PAIRED), 1, 0) for dl in (0, -1, 1)
     )
-    pl.semaphore_wait(barrier, rows * cols - 1 + jnp.where(far_left | far_right, far_rows, 0))
+    pl.semaphore_wait(barrier, rows * cols - 1 + jnp.where(far_left | far_right, far_rows, 0) + jnp.where(on_route, 2, 0))
 
     def load_copy(q, dt, to, j):
         into = LEFT if dt == 1 else RIGHT
@@ -197,7 +209,14 @@
     across = t + jnp.where(turn_left, -1, 1)
 
     def turn_copies():
-        pieces = [(dense, other), (s_v.at[1], s_other.at[0]), (s_v.at[3], s_other.at[1])]
+        rest = pl.ds(0, (16 - ROUTED) % 4 * SPAN)
+        whole = pl.ds(0, (16 - ROUTED) // 4)
+        pieces = [
+            (dense.at[(16 - ROUTED) // 4, rest], other.at[(16 - ROUTED) // 4, rest]),
+            (dense.at[whole], other.at[whole]),
+            (s_v.at[1], s_other.at[0]),
+            (s_v.at[3], s_other.at[1]),
+        ]
         return [
             pltpu.make_async_remote_copy(
                 src_ref=here,
@@ -212,6 +231,18 @@
 
     at_turn = paired & (turn_left | turn_right)
 
+    def route_copy(k, here):
+        i = 15 - k
+        piece = (i // 4, pl.ds(i % 4 * SPAN, SPAN))
+        return pltpu.make_async_remote_copy(
+            src_ref=here.at[piece],
+            dst_ref=other.at[piece],
+            send_sem=rsend.at[k],
+            recv_sem=rrecv.at[k],
+            device_id=(l, route_to),
+            device_id_type=MESH,
+        )
+
     def sends_load(q, dt):
         there = has_left if dt == -1 else has_right
         turn = turn_left if dt == -1 else turn_right
@@ -232,8 +263,18 @@
 
     @pl.when(at_turn)
     def _():
-        for copy in turn_copies()[::-1]:
+        for copy in turn_copies()[:1:-1]:
             copy.start()
+        for k in range(ROUTED):
+            route_copy(k, dense).start()
+        for copy in turn_copies()[1::-1]:
+            copy.start()
+
+    @pl.when(on_route & jnp.logical_not(at_turn))
+    def _():
+        for k in range(ROUTED):
+            route_copy(k, other).wait_recv()
+            route_copy(k, other).start()
 
     def product(q, window, matrix, b, start, blocks):
         operand = jnp.concatenate([ext[q, window + c] for c in blocks], axis=1)
@@ -343,6 +384,8 @@
             def _():
                 for copy in turn_copies():
                     copy.wait_recv()
+                for k in range(ROUTED):
+                    route_copy(k, dense).wait_recv()
 
             window = jnp.where(turn_left, FAR_LEFT, OWN)
             into = jnp.where(turn_left, LEFT, RIGHT)
@@ -443,6 +486,11 @@
     def _():
         for copy in turn_copies():
             copy.wait_send()
+
+    @pl.when(on_route)
+    def _():
+        for k in range(ROUTED):
+            route_copy(k, dense).wait_send()
 
     @pl.when(paired & (far_left & (w == 1) | far_right & (w == TURN - 2)))
     def _():
@@ -513,8 +561,10 @@
             dma((4, 2)),
             dma((4,)),
             dma((4,)),
-            dma((3,)),
-            dma((3,)),
+            dma((4,)),
+            dma((4,)),
+            dma((ROUTED,)),
+            dma((ROUTED,)),
             dma((2, 4)),
         ],
         compiler_params=pltpu.CompilerParams(

time: 74.1 us -> 69.6 us (0.939)
  Pallas kernels: 72 us -> 67.5 us
    pallas_call x1, Pallas kernels: 72 us -> 67.5 us  [per_device(): pl.pallas_call(functools.partial(kernel, layers, tiles), out_shape=(field...]
where the time goes in v4:
time: 69.6 us; the launch traced here: 69.5 us
  Pallas kernels  67.5 us (97%)
  local copies, waits for them, and re-layouts  1.41 us (2%)
    pallas_call x1, Pallas kernels, per_device(): pl.pallas_call(functools.partial(kernel, layers, tiles), out_shape=(field...  67.5 us
    unnamed x2, local copies, waits for them, and re-layouts  1.41 us

profile of v4, /device:TPU:127, one launch (start us, length us, event | category | flops | bytes accessed | tf_op | source)
XLA Modules:
  0.0 69.5 jit_solution(7501789993398389324)
XLA Ops:
  0.6 67.5 %shard_map.59 = (f32[4,2,64,128]{3,2,1,0:T(8,128)S(1)}, f32[4,2,64,128]{3,2,1,0:T(8,128)S(1)}) custom-call(f32[4,2,64,128]{3,2,1,0:T(8,128)} %bitcast.9, f32[4,8,128]{2,1,0:T(8,128)} %bitcast.10, bf16[4,8,2,128,128]{4,3,2,1,0:T(8,128)(2,1)} %bitcast.8, s32[4,8]{1,0:T(4,128)} %bitcast.11), custom_call_target="tpu_custom_call" | custom-call | tf_op jit(solution)/shard_map/pallas_call | solution.py:534
  68.1 0.7 %copy.10 = f32[4,2,16,1,512]{4,3,2,1,0:T(1,128)} copy(f32[4,2,16,1,512]{4,3,2,1,0:T(1,128)S(1)} %bitcast.7) | data formatting | bytes 524288
  68.8 0.7 %copy.11 = f32[4,2,16,1,512]{4,3,2,1,0:T(1,128)} copy(f32[4,2,16,1,512]{4,3,2,1,0:T(1,128)S(1)} %bitcast.6) | data formatting | bytes 524288

commit v5 on v4

--- a/solution.py
+++ b/solution.py
@@ -13,35 +13,35 @@
 TURN = 8
 PAIRED = 1
 ROUTE = {7: (-2, -3), 4: (3, 6), 2: (-6, -2), 0: (2, 3), 3: (-3, -6), 5: (6, 2)}
-ROUTED = 5
+ROUTED = 6
 SPAN = 288
 FAR_LEFT, LEFT, OWN, RIGHT, FAR_RIGHT = 0, 4, 8, 12, 16
 CUTS = 2
 PIECE = NB // CUTS
-REMOTE = 5
-
-
-def stages(b):
-    return [
-        [c for c in range(4 - PIECE * (j + 1), 4 - PIECE * j) if c >= b]
-        + [8 + c for c in range(PIECE * j, PIECE * (j + 1)) if c <= b]
-        for j in range(CUTS)
-    ]
-
-
-def places(b):
-    return [c for stage in stages(b) for c in stage] + [4, 5, 6, 7]
+
+
+def stages(v):
+    return [[c for c in range(4 - PIECE * (j + 1), 4 - PIECE * j) if c >= v] for j in range(CUTS)]
+
+
+def places(v):
+    return [c for stage in stages(v) for c in stage] + list(range(8, 9 + v)) + [4, 5, 6, 7]
 
 
 def kernel(
     layers, tiles, src, shift, fro, columns, sol, res,
-    s_v, sh_v, fro_v, col, dense, other, s_other, ext, xo, xh, xlay, xs, acc, sol_v, res_v,
-    lsem, lsend, lrecv, fsend, frecv, xsend, xrecv, csend, crecv, gsend, grecv, rsend, rrecv, osem,
+    s_v, sh_v, fro_v, col, dense, other, s_other, ext, xo, xh, xlay, xs, acc, other_acc, sol_v, res_v,
+    lsem, lsend, lrecv, esend, erecv, fsend, frecv, xsend, xrecv, csend, crecv, gsend, grecv, rsend, rrecv, osem,
 ):
     l, t = lax.axis_index("layer"), lax.axis_index("tile")
     first, last = l == 0, l == layers - 1
     has_left, has_right = t > 0, t < tiles - 1
     w = lax.rem(t, TURN)
+    plain = lax.rem(t, 2) == 0
+    where_is = [jnp.where(plain, p, 19 - p) for p in range(16)]
+    row_of = [jnp.where(plain, b, 3 - b) for b in range(NB)]
+    late = jnp.where(plain, -1, 1)
+    has_late = jnp.where(plain, t, tiles - 1 - t) > 0
     turn_left, turn_right = has_left & (w == 0), has_right & (w == TURN - 1)
     far_left = (t > 1) & (w <= 1)
     far_right = (t < tiles - 2) & (w >= TURN - 2)
@@ -79,7 +79,7 @@
     load_c = pltpu.make_async_copy(columns, col, lsem.at[0])
     load_s = pltpu.make_async_copy(src, s_v.at[pl.ds(0, 4)], lsem.at[1])
     load_w = pltpu.make_async_copy(shift, sh_v, lsem.at[2])
-    load_f = [pltpu.make_async_copy(fro.at[b], fro_v.at[b], lsem.at[3 + b]) for b in range(NB)]
+    load_f = [pltpu.make_async_copy(fro.at[row_of[v]], fro_v.at[v], lsem.at[3 + v]) for v in range(NB)]
     load_c.start()
     load_f[0].start()
     load_s.start()
@@ -110,19 +110,21 @@
         return s_v[q, part, pl.ds(b, 16, stride=4), :]
 
     load_c.wait()
-    for b in range(NB):
-        load_f[b].wait()
-        hit = [[col[b, k] == c - b for k in range(8)] for c in places(b)]
-
-        def densify(i, carry, b=b, hit=hit):
+    for v in range(NB):
+        load_f[v].wait()
+        hit = [
+            [col[row_of[v], k] == jnp.where(plain, c - v, 8 + v - c) for k in range(8)] for c in places(v)
+        ]
+
+        def densify(i, carry, v=v, hit=hit):
             r = pl.multiple_of(i * 16, 16)
             for part in range(2):
-                blocks = [fro_v[b, k, part, pl.ds(r, 16), :].astype(F32) for k in range(8)]
+                blocks = [fro_v[v, k, part, pl.ds(r, 16), :].astype(F32) for k in range(8)]
                 for place in range(9):
                     total = jnp.where(hit[place][0], blocks[0], 0.0)
                     for k in range(1, 8):
                         total = total + jnp.where(hit[place][k], blocks[k], 0.0)
-                    dense[b, pl.ds(pl.multiple_of(place * 128 + r, 16), 16), part * 128 : part * 128 + 128] = total.astype(BF16)
+                    dense[v, pl.ds(pl.multiple_of(place * 128 + r, 16), 16), part * 128 : part * 128 + 128] = total.astype(BF16)
             return carry
 
         lax.fori_loop(0, 8, densify, 0)
@@ -142,15 +144,24 @@
     )
     pl.semaphore_wait(barrier, rows * cols - 1 + jnp.where(far_left | far_right, far_rows, 0) + jnp.where(on_route, 2, 0))
 
-    def load_copy(q, dt, to, j):
-        into = LEFT if dt == 1 else RIGHT
-        c = 4 - PIECE * (j + 1) if dt == 1 else PIECE * j
+    def late_copy(q, to, j):
+        c = jnp.where(plain, PIECE * j, 4 - PIECE * (j + 1))
         return pltpu.make_async_remote_copy(
             src_ref=ext.at[q, pl.ds(OWN + c, PIECE)],
-            dst_ref=ext.at[lax.rem(q, 4), pl.ds(into + c, PIECE)],
-            send_sem=lsend.at[q, (1 + dt) // 2, j],
-            recv_sem=lrecv.at[lax.rem(q, 4), (1 - dt) // 2, j],
-            device_id=(to, t + dt),
+            dst_ref=ext.at[lax.rem(q, 4), pl.ds(jnp.where(plain, RIGHT, LEFT) + c, PIECE)],
+            send_sem=lsend.at[q, j],
+            recv_sem=lrecv.at[lax.rem(q, 4), j],
+            device_id=(to, t + late),
+            device_id_type=MESH,
+        )
+
+    def early_copy(q, to):
+        return pltpu.make_async_remote_copy(
+            src_ref=ext.at[q, pl.ds(OWN, 4)],
+            dst_ref=ext.at[lax.rem(q, 4), pl.ds(jnp.where(plain, LEFT, RIGHT), 4)],
+            send_sem=esend.at[q],
+            recv_sem=erecv.at[lax.rem(q, 4)],
+            device_id=(to, t - late),
             device_id_type=MESH,
         )
 
@@ -243,19 +254,17 @@
             device_id_type=MESH,
         )
 
-    def sends_load(q, dt):
-        there = has_left if dt == -1 else has_right
-        turn = turn_left if dt == -1 else turn_right
-        return there & jnp.logical_not(paired & turn & (lax.rem(q, 2) == 1))
-
-    for step in range(CUTS):
-        @pl.when(first & has_left)
-        def _():
-            load_copy(0, -1, l, step).start()
-
-        @pl.when(first & has_right)
-        def _():
-            load_copy(0, 1, l, step).start()
+    def late_moves(q):
+        return has_late & jnp.logical_not(at_turn & (lax.rem(q, 2) == 1))
+
+    @pl.when(first & has_late)
+    def _():
+        for j in range(CUTS):
+            late_copy(0, l, j).start()
+
+    @pl.when(first)
+    def _():
+        early_copy(0, l).start()
 
     @pl.when(jnp.logical_not(first))
     def _():
@@ -276,11 +285,11 @@
             route_copy(k, other).wait_recv()
             route_copy(k, other).start()
 
-    def product(q, window, matrix, b, start, blocks):
-        operand = jnp.concatenate([ext[q, window + c] for c in blocks], axis=1)
+    def product(q, blocks, matrix, v, start):
+        operand = jnp.concatenate([ext[q, where_is[p]] for p in blocks], axis=1)
         return jnp.dot(
             operand,
-            matrix[b, start * 128 : (start + len(blocks)) * 128],
+            matrix[v, start * 128 : (start + len(blocks)) * 128],
             preferred_element_type=F32,
         )
 
@@ -320,65 +329,13 @@
         def _():
             own_copy().wait_recv()
 
-        for b in range(NB):
-            acc[b] = product(q, LEFT, dense, b, REMOTE, [4, 5, 6, 7])
-
-        @pl.when((q == 3) & jnp.logical_not(last))
-        def _():
-            source_copy().wait_recv()
-
-        for j in range(CUTS):
-            @pl.when(sends_load(q, -1))
-            def _():
-                load_copy(q, 1, l, j).wait_recv()
-
-            @pl.when(sends_load(q, 1))
-            def _():
-                load_copy(q, -1, l, j).wait_recv()
-
-            for b in range(NB):
-                needs = stages(b)[j]
-                if not needs:
-                    continue
-                start = sum(len(s) for s in stages(b)[:j])
-                total = acc[b] + product(q, LEFT, dense, b, start, needs)
-                if any(stages(b)[j + 1 :]):
-                    acc[b] = total
-                    continue
-                re, im = combine(total)
-                ext[q + 1, OWN + b, 0:16] = (source(q + 1, 0, b) + re).astype(BF16)
-                ext[q + 1, OWN + b, 16:32] = (source(q + 1, 1, b) + im).astype(BF16)
-                xs[q + 1, 0, b] = re
-                xs[q + 1, 1, b] = im
-
-        handing = (q == 3) & jnp.logical_not(last)
-        onward = (q < 3) | jnp.logical_not(last)
-        to = l + q // 3
-
-        for step in range(CUTS):
-            @pl.when(onward & (handing & has_left | (q < 3) & sends_load(q + 1, -1)))
-            def _():
-                load_copy(q + 1, -1, to, step).start()
-
-            @pl.when(onward & (handing & has_right | (q < 3) & sends_load(q + 1, 1)))
-            def _():
-                load_copy(q + 1, 1, to, step).start()
-
-        @pl.when(handing)
-        def _():
-            own_copy().start()
-
-        sends_far = (handing & (l + 1 >= PAIRED)) | ((q == 1) & paired)
-
-        @pl.when(sends_far & far_left & (w == 1))
-        def _():
-            far_copy(q + 1, -2, to).start()
-
-        @pl.when(sends_far & far_right & (w == TURN - 2))
-        def _():
-            far_copy(q + 1, 2, to).start()
-
-        @pl.when(at_turn & (lax.rem(q, 2) == 0))
+        early_copy(q, l).wait_recv()
+        for v in range(NB):
+            acc[v] = product(q, [4 + c for c in places(v)[4 - v :]], dense, v, 4 - v)
+
+        doubles = at_turn & (lax.rem(q, 2) == 0)
+
+        @pl.when(doubles)
         def _():
             @pl.when(q == 0)
             def _():
@@ -387,22 +344,68 @@
                 for k in range(ROUTED):
                     route_copy(k, dense).wait_recv()
 
-            window = jnp.where(turn_left, FAR_LEFT, OWN)
+            for v in range(NB):
+                other_acc[v] = product(q, [11 - c for c in places(v)[: 4 - v]], other, v, 0)
+
+        @pl.when((q == 3) & jnp.logical_not(last))
+        def _():
+            source_copy().wait_recv()
+
+        for j in range(CUTS):
+            @pl.when(late_moves(q))
+            def _():
+                late_copy(q, l, j).wait_recv()
+
+            for v in range(NB):
+                needs = stages(v)[j]
+                if needs:
+                    start = sum(len(s) for s in stages(v)[:j])
+                    acc[v] += product(q, [4 + c for c in needs], dense, v, start)
+
+        for b in range(NB):
+            re, im = combine(acc[row_of[b]])
+            ext[q + 1, OWN + b, 0:16] = (source(q + 1, 0, b) + re).astype(BF16)
+            ext[q + 1, OWN + b, 16:32] = (source(q + 1, 1, b) + im).astype(BF16)
+            xs[q + 1, 0, b] = re
+            xs[q + 1, 1, b] = im
+
+        handing = (q == 3) & jnp.logical_not(last)
+        onward = (q < 3) | jnp.logical_not(last)
+        to = l + q // 3
+
+        @pl.when((handing & has_late) | ((q < 3) & late_moves(q + 1)))
+        def _():
+            for j in range(CUTS):
+                late_copy(q + 1, to, j).start()
+
+        @pl.when(onward)
+        def _():
+            early_copy(q + 1, to).start()
+
+        @pl.when(handing)
+        def _():
+            own_copy().start()
+
+        sends_far = (handing & (l + 1 >= PAIRED)) | ((q == 1) & paired)
+
+        @pl.when(sends_far & far_left & (w == 1))
+        def _():
+            far_copy(q + 1, -2, to).start()
+
+        @pl.when(sends_far & far_right & (w == TURN - 2))
+        def _():
+            far_copy(q + 1, 2, to).start()
+
+        @pl.when(doubles)
+        def _():
+            far_copy(q, 2, l).wait_recv()
+
+            for v in range(NB):
+                other_acc[v] += product(q, [11 - c for c in places(v)[4 - v :]], other, v, 4 - v)
+
             into = jnp.where(turn_left, LEFT, RIGHT)
             for b in range(NB):
-                acc[b] = product(q, window, other, b, REMOTE, [4, 5, 6, 7])
-
-            @pl.when(turn_left)
-            def _():
-                far_copy(q, 2, l).wait_recv()
-
-            @pl.when(turn_right)
-            def _():
-                far_copy(q, -2, l).wait_recv()
-
-            for b in range(NB):
-                total = acc[b] + product(q, window, other, b, 0, places(b)[:REMOTE])
-                re, im = combine(total)
+                re, im = combine(other_acc[3 - row_of[b]])
                 there = [s_other[q // 2, part, pl.ds(b, 16, stride=4), :] for part in range(2)]
                 ext[q + 1, into + b, 0:16] = (there[0] + re).astype(BF16)
                 ext[q + 1, into + b, 16:32] = (there[1] + im).astype(BF16)
@@ -463,14 +466,14 @@
 
     lax.fori_loop(0, 4, residual, 0)
 
-    for c in range(CUTS):
-        @pl.when(first & has_left)
-        def _():
-            load_copy(0, -1, l, c).wait_send()
-
-        @pl.when(first & has_right)
-        def _():
-            load_copy(0, 1, l, c).wait_send()
+    @pl.when(first & has_late)
+    def _():
+        for j in range(CUTS):
+            late_copy(0, l, j).wait_send()
+
+    @pl.when(first)
+    def _():
+        early_copy(0, l).wait_send()
 
     @pl.when(jnp.logical_not(first))
     def _():
@@ -510,14 +513,15 @@
             x_copy(q, 1).wait_send()
 
         handing = (q == 3) & jnp.logical_not(last)
-        for c in range(CUTS):
-            @pl.when(handing & has_left | (q < 3) & sends_load(q + 1, -1))
-            def _():
-                load_copy(q + 1, -1, l, c).wait_send()
-
-            @pl.when(handing & has_right | (q < 3) & sends_load(q + 1, 1))
-            def _():
-                load_copy(q + 1, 1, l, c).wait_send()
+
+        @pl.when((handing & has_late) | ((q < 3) & late_moves(q + 1)))
+        def _():
+            for j in range(CUTS):
+                late_copy(q + 1, l, j).wait_send()
+
+        @pl.when((q < 3) | handing)
+        def _():
+            early_copy(q + 1, l).wait_send()
 
         pltpu.make_async_copy(sol_v.at[q], sol.at[q], osem.at[0, q]).wait()
         pltpu.make_async_copy(res_v.at[q], res.at[q], osem.at[1, q]).wait()
@@ -550,11 +554,14 @@
             pltpu.VMEM((2, 4, 32, 128), BF16),
             pltpu.VMEM((6, 2, 4, 16, 128), F32),
             pltpu.VMEM((4, 32, 256), F32),
+            pltpu.VMEM((4, 32, 256), F32),
             pltpu.VMEM((4, 2, 64, 128), F32),
             pltpu.VMEM((4, 2, 64, 128), F32),
             dma((7,)),
-            dma((5, 2, CUTS)),
-            dma((4, 2, CUTS)),
+            dma((5, CUTS)),
+            dma((4, CUTS)),
+            dma((5,)),
+            dma((4,)),
             dma((5,)),
             dma((4,)),
             dma((4, 2)),

time: 69.6 us -> 67.2 us (0.966)
  Pallas kernels: 67.5 us -> 65.1 us
    pallas_call x1, Pallas kernels: 67.5 us -> 65.1 us  [per_device(): pl.pallas_call(functools.partial(kernel, layers, tiles), out_shape=(field...]
where the time goes in v5:
time: 67.2 us; the launch traced here: 67.1 us
  Pallas kernels  65.1 us (97%)
  local copies, waits for them, and re-layouts  1.41 us (2%)
    pallas_call x1, Pallas kernels, per_device(): pl.pallas_call(functools.partial(kernel, layers, tiles), out_shape=(field...  65.1 us
    unnamed x2, local copies, waits for them, and re-layouts  1.41 us

profile of v5, /device:TPU:127, one launch (start us, length us, event | category | flops | bytes accessed | tf_op | source)
XLA Modules:
  0.0 67.1 jit_solution(18350555279672528650)
XLA Ops:
  0.6 65.1 %shard_map.59 = (f32[4,2,64,128]{3,2,1,0:T(8,128)S(1)}, f32[4,2,64,128]{3,2,1,0:T(8,128)S(1)}) custom-call(f32[4,2,64,128]{3,2,1,0:T(8,128)} %bitcast.9, f32[4,8,128]{2,1,0:T(8,128)} %bitcast.10, bf16[4,8,2,128,128]{4,3,2,1,0:T(8,128)(2,1)} %bitcast.8, s32[4,8]{1,0:T(4,128)} %bitcast.11), custom_call_target="tpu_custom_call" | custom-call | tf_op jit(solution)/shard_map/pallas_call | solution.py:538
  65.7 0.7 %copy.10 = f32[4,2,16,1,512]{4,3,2,1,0:T(1,128)} copy(f32[4,2,16,1,512]{4,3,2,1,0:T(1,128)S(1)} %bitcast.7) | data formatting | bytes 524288
  66.4 0.7 %copy.11 = f32[4,2,16,1,512]{4,3,2,1,0:T(1,128)} copy(f32[4,2,16,1,512]{4,3,2,1,0:T(1,128)S(1)} %bitcast.6) | data formatting | bytes 524288

commit v6 on v5

--- a/solution.py
+++ b/solution.py
@@ -18,6 +18,7 @@
 FAR_LEFT, LEFT, OWN, RIGHT, FAR_RIGHT = 0, 4, 8, 12, 16
 CUTS = 2
 PIECE = NB // CUTS
+REMOTE = 5
 
 
 def stages(v):
@@ -30,8 +31,8 @@
 
 def kernel(
     layers, tiles, src, shift, fro, columns, sol, res,
-    s_v, sh_v, fro_v, col, dense, other, s_other, ext, xo, xh, xlay, xs, acc, other_acc, sol_v, res_v,
-    lsem, lsend, lrecv, esend, erecv, fsend, frecv, xsend, xrecv, csend, crecv, gsend, grecv, rsend, rrecv, osem,
+    s_v, sh_v, fro_v, col, dense, other, s_other, ext, xo, xh, xlay, xs, acc, other_acc,
+    lsem, lsend, lrecv, esend, erecv, fsend, frecv, xsend, xrecv, csend, crecv, gsend, grecv, rsend, rrecv,
 ):
     l, t = lax.axis_index("layer"), lax.axis_index("tile")
     first, last = l == 0, l == layers - 1
@@ -53,23 +54,16 @@
     route_to = t + sum(jnp.where(w == place, ROUTE[place][1], 0) for place in ROUTE)
 
     barrier = pltpu.get_barrier_semaphore()
-    for dl in (0, -1, 1):
-        layer_there = (l + dl >= 0) & (l + dl < layers)
-        for dt in (-1, 0, 1):
-            if dl == 0 and dt == 0:
-                continue
-            there = layer_there & (t + dt >= 0) & (t + dt < tiles)
-
-            @pl.when(there)
-            def _():
-                pl.semaphore_signal(barrier, inc=1, device_id=(l + dl, t + dt), device_id_type=MESH)
-
-    for dl in (0, -1, 1):
-        layer_there = (l + dl >= 0) & (l + dl < layers)
-
-        @pl.when(layer_there & (far_left | far_right) & (l + max(dl, 0) >= PAIRED))
-        def _():
-            pl.semaphore_signal(barrier, inc=1, device_id=(l + dl, t + far), device_id_type=MESH)
+    for there, dl, dt in (
+        (has_left, 0, -1),
+        (has_right, 0, 1),
+        (paired & (far_left | far_right), 0, far),
+        (jnp.logical_not(first), -1, 0),
+        (jnp.logical_not(last), 1, 0),
+    ):
+        @pl.when(there)
+        def _():
+            pl.semaphore_signal(barrier, inc=1, device_id=(l + dl, t + dt), device_id_type=MESH)
 
     @pl.when(on_route)
     def _():
@@ -137,12 +131,12 @@
             ext[0, OWN + b, 0:16] = source(0, 0, b).astype(BF16)
             ext[0, OWN + b, 16:32] = source(0, 1, b).astype(BF16)
 
-    rows = jnp.where(first | last, 2, 3)
-    cols = jnp.where(has_left & has_right, 3, 2)
-    far_rows = sum(
-        jnp.where((l + dl >= 0) & (l + dl < layers) & (l + max(dl, 0) >= PAIRED), 1, 0) for dl in (0, -1, 1)
+    one = lambda there: jnp.where(there, 1, 0)
+    pl.semaphore_wait(
+        barrier,
+        one(has_left) + one(has_right) + one(paired & (far_left | far_right))
+        + one(jnp.logical_not(first)) + one(jnp.logical_not(last)) + 2 * one(on_route),
     )
-    pl.semaphore_wait(barrier, rows * cols - 1 + jnp.where(far_left | far_right, far_rows, 0) + jnp.where(on_route, 2, 0))
 
     def late_copy(q, to, j):
         c = jnp.where(plain, PIECE * j, 4 - PIECE * (j + 1))
@@ -321,17 +315,23 @@
 
         for b in range(NB):
             for part in range(2):
-                sol_v[q, part, pl.ds(b, 16, stride=4), :] = xs[q + 1, part, b]
-        pltpu.make_async_copy(sol_v.at[q], sol.at[q], osem.at[0, q]).start()
+                sol[q, part, pl.ds(b, 16, stride=4), :] = xs[q + 1, part, b]
 
     def plane(q, carry):
         @pl.when(jnp.logical_not(first) & (q == 0))
         def _():
             own_copy().wait_recv()
 
-        early_copy(q, l).wait_recv()
-        for v in range(NB):
-            acc[v] = product(q, [4 + c for c in places(v)[4 - v :]], dense, v, 4 - v)
+        behind = at_turn & (lax.rem(q, 2) == 1)
+
+        def begin(q):
+            early_copy(q, l).wait_recv()
+            for v in range(NB):
+                acc[v] = product(q, [4 + c for c in places(v)[4 - v :]], dense, v, 4 - v)
+
+        @pl.when(jnp.logical_not(behind))
+        def _():
+            begin(q)
 
         doubles = at_turn & (lax.rem(q, 2) == 0)
 
@@ -351,23 +351,39 @@
         def _():
             source_copy().wait_recv()
 
-        for j in range(CUTS):
-            @pl.when(late_moves(q))
-            def _():
-                late_copy(q, l, j).wait_recv()
-
-            for v in range(NB):
-                needs = stages(v)[j]
-                if needs:
-                    start = sum(len(s) for s in stages(v)[:j])
-                    acc[v] += product(q, [4 + c for c in needs], dense, v, start)
-
-        for b in range(NB):
-            re, im = combine(acc[row_of[b]])
-            ext[q + 1, OWN + b, 0:16] = (source(q + 1, 0, b) + re).astype(BF16)
-            ext[q + 1, OWN + b, 16:32] = (source(q + 1, 1, b) + im).astype(BF16)
+        def finish(v):
+            b = row_of[v]
+            re, im = combine(acc[v])
+            ext[q + 1, OWN + b, 0:16] = (s_v[q + 1, 0, pl.ds(b, 16, stride=4), :] + re).astype(BF16)
+            ext[q + 1, OWN + b, 16:32] = (s_v[q + 1, 1, pl.ds(b, 16, stride=4), :] + im).astype(BF16)
             xs[q + 1, 0, b] = re
             xs[q + 1, 1, b] = im
+
+        @pl.when(behind)
+        def _():
+            for v in range(NB):
+                acc[v] += product(q, [4 + c for c in places(v)[: 4 - v]], dense, v, 0)
+            for v in range(PIECE, NB):
+                finish(v)
+
+        @pl.when(jnp.logical_not(behind))
+        def _():
+            for j in range(CUTS):
+                @pl.when(has_late)
+                def _():
+                    late_copy(q, l, j).wait_recv()
+
+                for v in range(NB):
+                    needs = stages(v)[j]
+                    if needs:
+                        start = sum(len(s) for s in stages(v)[:j])
+                        acc[v] += product(q, [4 + c for c in needs], dense, v, start)
+                if j == 0:
+                    for v in range(PIECE, NB):
+                        finish(v)
+
+        for v in range(PIECE):
+            finish(v)
 
         handing = (q == 3) & jnp.logical_not(last)
         onward = (q < 3) | jnp.logical_not(last)
@@ -398,10 +414,12 @@
 
         @pl.when(doubles)
         def _():
+            begin(q + 1)
+            for v in range(NB):
+                other_acc[v] += product(q, [11 - c for c in places(v)[REMOTE:]], other, v, REMOTE)
             far_copy(q, 2, l).wait_recv()
-
             for v in range(NB):
-                other_acc[v] += product(q, [11 - c for c in places(v)[4 - v :]], other, v, 4 - v)
+                other_acc[v] += product(q, [11 - c for c in places(v)[4 - v : REMOTE]], other, v, 4 - v)
 
             into = jnp.where(turn_left, LEFT, RIGHT)
             for b in range(NB):
@@ -460,8 +478,7 @@
                 beside = beside + xh[q, 0, b, half].astype(F32) + xh[q, 1, b, half].astype(F32)
                 cross = s_im * x[1] if part == 0 else -(s_im * x[0])
                 value = s_re * x[part] + cross - beside
-                res_v[q, part, pl.ds(b, 16, stride=4), :] = source(q, part, b) - value
-        pltpu.make_async_copy(res_v.at[q], res.at[q], osem.at[1, q]).start()
+                res[q, part, pl.ds(b, 16, stride=4), :] = source(q, part, b) - value
         return carry
 
     lax.fori_loop(0, 4, residual, 0)
@@ -523,23 +540,31 @@
         def _():
             early_copy(q + 1, l).wait_send()
 
-        pltpu.make_async_copy(sol_v.at[q], sol.at[q], osem.at[0, q]).wait()
-        pltpu.make_async_copy(res_v.at[q], res.at[q], osem.at[1, q]).wait()
         return carry
 
     lax.fori_loop(0, 4, drain, 0)
 
 
+def write_results(sol, res, sol_out, res_out, sem):
+    copies = [
+        pltpu.make_async_copy(sol, sol_out, sem.at[0]),
+        pltpu.make_async_copy(res, res_out, sem.at[1]),
+    ]
+    for copy in copies:
+        copy.start()
+    for copy in copies:
+        copy.wait()
+
+
 def per_device(layers, tiles, source_field, wave_shift, frontal_blocks, block_columns):
-    field = jax.ShapeDtypeStruct((4, 2, 64, 128), F32)
+    field = pltpu.VMEM((4, 2, 64, 128), F32)
     hbm = pl.BlockSpec(memory_space=pltpu.HBM)
-    anywhere = pl.BlockSpec(memory_space=pl.ANY)
     dma = pltpu.SemaphoreType.DMA
     sol, res = pl.pallas_call(
         functools.partial(kernel, layers, tiles),
         out_shape=(field, field),
         in_specs=[hbm, hbm, hbm, hbm],
-        out_specs=(anywhere, anywhere),
+        out_specs=(pl.BlockSpec(memory_space=pltpu.VMEM),) * 2,
         scratch_shapes=[
             pltpu.VMEM((5, 2, 64, 128), F32),
             pltpu.VMEM((4, 8, 128), F32),
@@ -555,8 +580,6 @@
             pltpu.VMEM((6, 2, 4, 16, 128), F32),
             pltpu.VMEM((4, 32, 256), F32),
             pltpu.VMEM((4, 32, 256), F32),
-            pltpu.VMEM((4, 2, 64, 128), F32),
-            pltpu.VMEM((4, 2, 64, 128), F32),
             dma((7,)),
             dma((5, CUTS)),
             dma((4, CUTS)),
@@ -572,7 +595,6 @@
             dma((4,)),
             dma((ROUTED,)),
             dma((ROUTED,)),
-            dma((2, 4)),
         ],
         compiler_params=pltpu.CompilerParams(
             collective_id=0, has_side_effects=True, vmem_limit_bytes=32 * 1024 * 1024
@@ -588,6 +610,16 @@
             )
         ]
     )
+    whole = jax.ShapeDtypeStruct((4, 2, 64, 128), F32)
+    out = pl.BlockSpec(memory_space=pltpu.HBM)
+    sol, res = pl.pallas_call(
+        write_results,
+        out_shape=(whole, whole),
+        in_specs=[pl.BlockSpec(memory_space=pltpu.VMEM)] * 2,
+        out_specs=(out, out),
+        scratch_shapes=[dma((2,))],
+        compiler_params=pltpu.CompilerParams(vmem_limit_bytes=8 * 1024 * 1024),
+    )(*[pltpu.with_memory_space_constraint(result, pltpu.VMEM) for result in (sol, res)])
     return sol.reshape(4, 2, 16, 1, 512), res.reshape(4, 2, 16, 1, 512)
 
 

time: 67.2 us -> 65.7 us (0.978)
  local copies, waits for them, and re-layouts: 1.41 us -> 0 us
    unnamed x2 -> x0, local copies, waits for them, and re-layouts: 1.41 us -> none
    pallas_call x1, Pallas kernels: 65.1 us -> 64.2 us  [per_device(): pl.pallas_call(functools.partial(kernel, layers, tiles), out_shape=(field...]
    pallas_call x0 -> x1, Pallas kernels: none -> 0.81 us  [per_device(): pl.pallas_call(write_results, out_shape=(whole, whole), in_specs=[pl.Bloc...]
where the time goes in v6:
time: 65.7 us; the launch traced here: 65.6 us
  Pallas kernels  65 us (99%)
    pallas_call x1, Pallas kernels, per_device(): pl.pallas_call(functools.partial(kernel, layers, tiles), out_shape=(field...  64.2 us

profile of v6, /device:TPU:127, one launch (start us, length us, event | category | flops | bytes accessed | tf_op | source)
XLA Modules:
  0.0 65.6 jit_solution(17512329916488085431)
XLA Ops:
  0.6 64.2 %shard_map.59 = (f32[4,2,64,128]{3,2,1,0:T(8,128)S(1)}, f32[4,2,64,128]{3,2,1,0:T(8,128)S(1)}) custom-call(f32[4,2,64,128]{3,2,1,0:T(8,128)} %bitcast.7, f32[4,8,128]{2,1,0:T(8,128)} %bitcast.8, bf16[4,8,2,128,128]{4,3,2,1,0:T(8,128)(2,1)} %bitcast.6, s32[4,8]{1,0:T(4,128)} %bitcast.9), custom_call_target="tpu_custom_call" | custom-call | tf_op jit(solution)/shard_map/pallas_call | solution.py:563
  64.8 0.8 %shard_map.60 = (f32[4,2,64,128]{3,2,1,0:T(8,128)}, f32[4,2,64,128]{3,2,1,0:T(8,128)}) custom-call(f32[4,2,64,128]{3,2,1,0:T(8,128)S(1)} %get-tuple-element.6.sol, f32[4,2,64,128]{3,2,1,0:T(8,128)S(1)} %get-tuple-element.7.res), custom_call_target="tpu_custom_call" | custom-call | tf_op jit(solution)/shard_map/pallas_call | solution.py:615

commit v7 on v6

--- a/solution.py
+++ b/solution.py
@@ -16,17 +16,11 @@
 ROUTED = 6
 SPAN = 288
 FAR_LEFT, LEFT, OWN, RIGHT, FAR_RIGHT = 0, 4, 8, 12, 16
-CUTS = 2
-PIECE = NB // CUTS
 REMOTE = 5
 
 
-def stages(v):
-    return [[c for c in range(4 - PIECE * (j + 1), 4 - PIECE * j) if c >= v] for j in range(CUTS)]
-
-
 def places(v):
-    return [c for stage in stages(v) for c in stage] + list(range(8, 9 + v)) + [4, 5, 6, 7]
+    return list(range(v, 4)) + list(range(8, 9 + v)) + [4, 5, 6, 7]
 
 
 def kernel(
@@ -138,13 +132,12 @@
         + one(jnp.logical_not(first)) + one(jnp.logical_not(last)) + 2 * one(on_route),
     )
 
-    def late_copy(q, to, j):
-        c = jnp.where(plain, PIECE * j, 4 - PIECE * (j + 1))
-        return pltpu.make_async_remote_copy(
-            src_ref=ext.at[q, pl.ds(OWN + c, PIECE)],
-            dst_ref=ext.at[lax.rem(q, 4), pl.ds(jnp.where(plain, RIGHT, LEFT) + c, PIECE)],
-            send_sem=lsend.at[q, j],
-            recv_sem=lrecv.at[lax.rem(q, 4), j],
+    def late_copy(q, to):
+        return pltpu.make_async_remote_copy(
+            src_ref=ext.at[q, pl.ds(OWN, 4)],
+            dst_ref=ext.at[lax.rem(q, 4), pl.ds(jnp.where(plain, RIGHT, LEFT), 4)],
+            send_sem=lsend.at[q],
+            recv_sem=lrecv.at[lax.rem(q, 4)],
             device_id=(to, t + late),
             device_id_type=MESH,
         )
@@ -248,13 +241,16 @@
             device_id_type=MESH,
         )
 
+    def x_moves(q, dt):
+        there, turn = (has_left, turn_left) if dt == -1 else (has_right, turn_right)
+        return there & jnp.logical_not(paired & last & turn & (q == 3))
+
     def late_moves(q):
         return has_late & jnp.logical_not(at_turn & (lax.rem(q, 2) == 1))
 
     @pl.when(first & has_late)
     def _():
-        for j in range(CUTS):
-            late_copy(0, l, j).start()
+        late_copy(0, l).start()
 
     @pl.when(first)
     def _():
@@ -297,11 +293,11 @@
             for part in range(2):
                 xo[q, b, part * 16 : part * 16 + 16] = xs[q + 1, part, b].astype(BF16)
 
-        @pl.when(has_left)
+        @pl.when(x_moves(q, -1))
         def _():
             x_copy(q, -1).start()
 
-        @pl.when(has_right)
+        @pl.when(x_moves(q, 1))
         def _():
             x_copy(q, 1).start()
 
@@ -316,6 +312,17 @@
         for b in range(NB):
             for part in range(2):
                 sol[q, part, pl.ds(b, 16, stride=4), :] = xs[q + 1, part, b]
+
+    def others_late(q):
+        for v in range(NB):
+            other_acc[v] = product(q, [11 - c for c in places(v)[: 4 - v]], other, v, 0)
+
+    def others_rest(q):
+        for v in range(NB):
+            other_acc[v] += product(q, [11 - c for c in places(v)[REMOTE:]], other, v, REMOTE)
+        far_copy(q, 2, l).wait_recv()
+        for v in range(NB):
+            other_acc[v] += product(q, [11 - c for c in places(v)[4 - v : REMOTE]], other, v, 4 - v)
 
     def plane(q, carry):
         @pl.when(jnp.logical_not(first) & (q == 0))
@@ -344,8 +351,7 @@
                 for k in range(ROUTED):
                     route_copy(k, dense).wait_recv()
 
-            for v in range(NB):
-                other_acc[v] = product(q, [11 - c for c in places(v)[: 4 - v]], other, v, 0)
+            others_late(q)
 
         @pl.when((q == 3) & jnp.logical_not(last))
         def _():
@@ -359,31 +365,18 @@
             xs[q + 1, 0, b] = re
             xs[q + 1, 1, b] = im
 
-        @pl.when(behind)
-        def _():
-            for v in range(NB):
-                acc[v] += product(q, [4 + c for c in places(v)[: 4 - v]], dense, v, 0)
-            for v in range(PIECE, NB):
-                finish(v)
-
-        @pl.when(jnp.logical_not(behind))
-        def _():
-            for j in range(CUTS):
-                @pl.when(has_late)
-                def _():
-                    late_copy(q, l, j).wait_recv()
-
-                for v in range(NB):
-                    needs = stages(v)[j]
-                    if needs:
-                        start = sum(len(s) for s in stages(v)[:j])
-                        acc[v] += product(q, [4 + c for c in needs], dense, v, start)
-                if j == 0:
-                    for v in range(PIECE, NB):
-                        finish(v)
-
-        for v in range(PIECE):
-            finish(v)
+        @pl.when(late_moves(q))
+        def _():
+            late_copy(q, l).wait_recv()
+
+        totals = [acc[v] + product(q, [4 + c for c in places(v)[: 4 - v]], dense, v, 0) for v in range(NB)]
+        for v in range(NB):
+            b = row_of[v]
+            re, im = combine(totals[v])
+            ext[q + 1, OWN + b, 0:16] = (s_v[q + 1, 0, pl.ds(b, 16, stride=4), :] + re).astype(BF16)
+            ext[q + 1, OWN + b, 16:32] = (s_v[q + 1, 1, pl.ds(b, 16, stride=4), :] + im).astype(BF16)
+            xs[q + 1, 0, b] = re
+            xs[q + 1, 1, b] = im
 
         handing = (q == 3) & jnp.logical_not(last)
         onward = (q < 3) | jnp.logical_not(last)
@@ -391,8 +384,7 @@
 
         @pl.when((handing & has_late) | ((q < 3) & late_moves(q + 1)))
         def _():
-            for j in range(CUTS):
-                late_copy(q + 1, to, j).start()
+            late_copy(q + 1, to).start()
 
         @pl.when(onward)
         def _():
@@ -402,7 +394,7 @@
         def _():
             own_copy().start()
 
-        sends_far = (handing & (l + 1 >= PAIRED)) | ((q == 1) & paired)
+        sends_far = (handing & (l + 1 >= PAIRED)) | ((q == 1) & paired) | ((q == 2) & paired & last)
 
         @pl.when(sends_far & far_left & (w == 1))
         def _():
@@ -415,12 +407,7 @@
         @pl.when(doubles)
         def _():
             begin(q + 1)
-            for v in range(NB):
-                other_acc[v] += product(q, [11 - c for c in places(v)[REMOTE:]], other, v, REMOTE)
-            far_copy(q, 2, l).wait_recv()
-            for v in range(NB):
-                other_acc[v] += product(q, [11 - c for c in places(v)[4 - v : REMOTE]], other, v, 4 - v)
-
+            others_rest(q)
             into = jnp.where(turn_left, LEFT, RIGHT)
             for b in range(NB):
                 re, im = combine(other_acc[3 - row_of[b]])
@@ -433,6 +420,15 @@
             publish(q)
             publish(q - 1)
 
+        @pl.when(at_turn & last & (q == 3))
+        def _():
+            others_late(q)
+            others_rest(q)
+            for b in range(NB):
+                re, im = combine(other_acc[3 - row_of[b]])
+                xh[3, jnp.where(turn_left, 0, 1), b, 0:16] = re.astype(BF16)
+                xh[3, jnp.where(turn_left, 0, 1), b, 16:32] = im.astype(BF16)
+
         return carry
 
     lax.fori_loop(0, 4, plane, 0)
@@ -455,11 +451,11 @@
     lane = lax.broadcasted_iota(jnp.int32, (16, 128), 1)
 
     def residual(q, carry):
-        @pl.when(has_left)
+        @pl.when(x_moves(q, -1))
         def _():
             x_copy(q, 1).wait_recv()
 
-        @pl.when(has_right)
+        @pl.when(x_moves(q, 1))
         def _():
             x_copy(q, -1).wait_recv()
 
@@ -485,8 +481,7 @@
 
     @pl.when(first & has_late)
     def _():
-        for j in range(CUTS):
-            late_copy(0, l, j).wait_send()
+        late_copy(0, l).wait_send()
 
     @pl.when(first)
     def _():
@@ -516,16 +511,20 @@
     def _():
         far_copy(2, 2, l).wait_send()
 
+        @pl.when(last)
+        def _():
+            far_copy(3, 2, l).wait_send()
+
     @pl.when(jnp.logical_not(last) & (l + 1 >= PAIRED) & (far_left & (w == 1) | far_right & (w == TURN - 2)))
     def _():
         far_copy(4, 2, l).wait_send()
 
     def drain(q, carry):
-        @pl.when(has_left)
+        @pl.when(x_moves(q, -1))
         def _():
             x_copy(q, -1).wait_send()
 
-        @pl.when(has_right)
+        @pl.when(x_moves(q, 1))
         def _():
             x_copy(q, 1).wait_send()
 
@@ -533,8 +532,7 @@
 
         @pl.when((handing & has_late) | ((q < 3) & late_moves(q + 1)))
         def _():
-            for j in range(CUTS):
-                late_copy(q + 1, l, j).wait_send()
+            late_copy(q + 1, l).wait_send()
 
         @pl.when((q < 3) | handing)
         def _():
@@ -581,8 +579,8 @@
             pltpu.VMEM((4, 32, 256), F32),
             pltpu.VMEM((4, 32, 256), F32),
             dma((7,)),
-            dma((5, CUTS)),
-            dma((4, CUTS)),
+            dma((5,)),
+            dma((4,)),
             dma((5,)),
             dma((4,)),
             dma((5,)),

time: 65.7 us -> 64.4 us (0.980)
  Pallas kernels: 65 us -> 63.6 us
    pallas_call x1, Pallas kernels: 64.2 us -> 62.8 us  [per_device(): pl.pallas_call(functools.partial(kernel, layers, tiles), out_shape=(field...]
where the time goes in v7:
time: 64.4 us; the launch traced here: 64.3 us
  Pallas kernels  63.6 us (99%)
    pallas_call x1, Pallas kernels, per_device(): pl.pallas_call(functools.partial(kernel, layers, tiles), out_shape=(field...  62.8 us

profile of v7, /device:TPU:127, one launch (start us, length us, event | category | flops | bytes accessed | tf_op | source)
XLA Modules:
  0.0 64.3 jit_solution(7434828223803530965)
XLA Ops:
  0.6 62.8 %shard_map.59 = (f32[4,2,64,128]{3,2,1,0:T(8,128)S(1)}, f32[4,2,64,128]{3,2,1,0:T(8,128)S(1)}) custom-call(f32[4,2,64,128]{3,2,1,0:T(8,128)} %bitcast.7, f32[4,8,128]{2,1,0:T(8,128)} %bitcast.8, bf16[4,8,2,128,128]{4,3,2,1,0:T(8,128)(2,1)} %bitcast.6, s32[4,8]{1,0:T(4,128)} %bitcast.9), custom_call_target="tpu_custom_call" | custom-call | tf_op jit(solution)/shard_map/pallas_call | solution.py:561
  63.5 0.8 %shard_map.60 = (f32[4,2,64,128]{3,2,1,0:T(8,128)}, f32[4,2,64,128]{3,2,1,0:T(8,128)}) custom-call(f32[4,2,64,128]{3,2,1,0:T(8,128)S(1)} %get-tuple-element.6.sol, f32[4,2,64,128]{3,2,1,0:T(8,128)S(1)} %get-tuple-element.7.res), custom_call_target="tpu_custom_call" | custom-call | tf_op jit(solution)/shard_map/pallas_call | solution.py:613

commit v8 on v7

--- a/solution.py
+++ b/solution.py
@@ -431,7 +431,8 @@
 
         return carry
 
-    lax.fori_loop(0, 4, plane, 0)
+    for q in range(4):
+        plane(q, 0)
 
     load_w.wait()
 
@@ -477,7 +478,8 @@
                 res[q, part, pl.ds(b, 16, stride=4), :] = source(q, part, b) - value
         return carry
 
-    lax.fori_loop(0, 4, residual, 0)
+    for q in range(4):
+        residual(q, 0)
 
     @pl.when(first & has_late)
     def _():
@@ -545,8 +547,9 @@
 
 def write_results(sol, res, sol_out, res_out, sem):
     copies = [
-        pltpu.make_async_copy(sol, sol_out, sem.at[0]),
-        pltpu.make_async_copy(res, res_out, sem.at[1]),
+        pltpu.make_async_copy(here.at[q], there.at[q], sem.at[i, q])
+        for q in range(4)
+        for i, (here, there) in enumerate(((sol, sol_out), (res, res_out)))
     ]
     for copy in copies:
         copy.start()
@@ -615,7 +618,7 @@
         out_shape=(whole, whole),
         in_specs=[pl.BlockSpec(memory_space=pltpu.VMEM)] * 2,
         out_specs=(out, out),
-        scratch_shapes=[dma((2,))],
+        scratch_shapes=[dma((2, 4))],
         compiler_params=pltpu.CompilerParams(vmem_limit_bytes=8 * 1024 * 1024),
     )(*[pltpu.with_memory_space_constraint(result, pltpu.VMEM) for result in (sol, res)])
     return sol.reshape(4, 2, 16, 1, 512), res.reshape(4, 2, 16, 1, 512)

time: 64.4 us -> 64.4 us (level)
  no operation moved by 1% of the time
where the time goes in v8:
time: 64.4 us; the launch traced here: 64.3 us
  Pallas kernels  63.6 us (99%)
    pallas_call x1, Pallas kernels, per_device(): pl.pallas_call(functools.partial(kernel, layers, tiles), out_shape=(field...  62.8 us

profile of v8, /device:TPU:127, one launch (start us, length us, event | category | flops | bytes accessed | tf_op | source)
XLA Modules:
  0.0 64.3 jit_solution(1184994275314020332)
XLA Ops:
  0.6 62.8 %shard_map.59 = (f32[4,2,64,128]{3,2,1,0:T(8,128)S(1)}, f32[4,2,64,128]{3,2,1,0:T(8,128)S(1)}) custom-call(f32[4,2,64,128]{3,2,1,0:T(8,128)} %bitcast.7, f32[4,8,128]{2,1,0:T(8,128)} %bitcast.8, bf16[4,8,2,128,128]{4,3,2,1,0:T(8,128)(2,1)} %bitcast.6, s32[4,8]{1,0:T(4,128)} %bitcast.9), custom_call_target="tpu_custom_call" | custom-call | tf_op jit(solution)/shard_map/pallas_call | solution.py:564
  63.4 0.9 %shard_map.60 = (f32[4,2,64,128]{3,2,1,0:T(8,128)}, f32[4,2,64,128]{3,2,1,0:T(8,128)}) custom-call(f32[4,2,64,128]{3,2,1,0:T(8,128)S(1)} %get-tuple-element.6.sol, f32[4,2,64,128]{3,2,1,0:T(8,128)S(1)} %get-tuple-element.7.res), custom_call_target="tpu_custom_call" | custom-call | tf_op jit(solution)/shard_map/pallas_call | solution.py:616

commit v9 on v8

--- a/solution.py
+++ b/solution.py
@@ -415,10 +415,14 @@
                 ext[q + 1, into + b, 0:16] = (there[0] + re).astype(BF16)
                 ext[q + 1, into + b, 16:32] = (there[1] + im).astype(BF16)
 
-        @pl.when(lax.rem(q, 2) == 1)
+        @pl.when(jnp.logical_not(at_turn) | (lax.rem(q, 2) == 1))
         def _():
             publish(q)
-            publish(q - 1)
+
+        if q % 2 == 1:
+            @pl.when(at_turn)
+            def _():
+                publish(q - 1)
 
         @pl.when(at_turn & last & (q == 3))
         def _():

time: 64.4 us -> 64.4 us (level)
  no operation moved by 1% of the time
where the time goes in v9:
time: 64.4 us; the launch traced here: 64.3 us
  Pallas kernels  63.6 us (99%)
    pallas_call x1, Pallas kernels, per_device(): pl.pallas_call(functools.partial(kernel, layers, tiles), out_shape=(field...  62.8 us

profile of v9, /device:TPU:127, one launch (start us, length us, event | category | flops | bytes accessed | tf_op | source)
XLA Modules:
  0.0 64.3 jit_solution(11815051671896446343)
XLA Ops:
  0.6 62.8 %shard_map.59 = (f32[4,2,64,128]{3,2,1,0:T(8,128)S(1)}, f32[4,2,64,128]{3,2,1,0:T(8,128)S(1)}) custom-call(f32[4,2,64,128]{3,2,1,0:T(8,128)} %bitcast.7, f32[4,8,128]{2,1,0:T(8,128)} %bitcast.8, bf16[4,8,2,128,128]{4,3,2,1,0:T(8,128)(2,1)} %bitcast.6, s32[4,8]{1,0:T(4,128)} %bitcast.9), custom_call_target="tpu_custom_call" | custom-call | tf_op jit(solution)/shard_map/pallas_call | solution.py:568
  63.4 0.9 %shard_map.60 = (f32[4,2,64,128]{3,2,1,0:T(8,128)}, f32[4,2,64,128]{3,2,1,0:T(8,128)}) custom-call(f32[4,2,64,128]{3,2,1,0:T(8,128)S(1)} %get-tuple-element.6.sol, f32[4,2,64,128]{3,2,1,0:T(8,128)S(1)} %get-tuple-element.7.res), custom_call_target="tpu_custom_call" | custom-call | tf_op jit(solution)/shard_map/pallas_call | solution.py:620
